TPU v7x, 512 devices: a whole 4x4x16 slice. The times are simulated.
512 devices in a mesh: gx: 32 (over z, x_lo), gy: 16 (over y, x_hi, core).
Axes of the slice: x: 4 (x_hi: 2, x_lo: 2; x = x_hi * 2 + x_lo), y: 4, z: 16, core: 2. Of those that a mesh axis runs over, the one named last changes fastest.
Arguments:
- cell_offset: float32 [3, 64, 32, 2048], P(None, 'gx', 'gy'), may hold values from 0 to 1
- velocity: float32 [3, 64, 32, 2048], P(None, 'gx', 'gy'), may hold values from -6 to 6
- affine: float32 [9, 64, 32, 2048], P(None, 'gx', 'gy'), may hold values from -3 to 3
- cell_index: int32 [64, 32, 2048], P('gx', 'gy'), may hold values from 0 to 63
- counts: int32 [64, 32, 32], P('gx', 'gy'), may hold values from 16 to 64, as said below
- cell_flags: int32 [256, 128, 128], P('gx', 'gy'), may hold values from 0 to 2, as said below
- old_pressure: float32 [256, 128, 128], P('gx', 'gy'), may hold values from -6 to 6
- destination: int32 [64, 32, 2048], P('gx', 'gy'), may hold values from 0 to 8, as said below
- dest_slot: int32 [64, 32, 2048], P('gx', 'gy'), may hold values from 0 to 255, as said below
Outputs:
- new_offset: float32 [3, 64, 32, 2048], P(None, 'gx', 'gy')
- new_velocity: float32 [3, 64, 32, 2048], P(None, 'gx', 'gy')
- new_affine: float32 [9, 64, 32, 2048], P(None, 'gx', 'gy')
- pressure: float32 [256, 128, 128], P('gx', 'gy')
- received: float32 [15, 8, 32, 4096], P(None, None, 'gx', 'gy')
Inputs may be any that keep to these rules, and one draw needn't show every extreme that they name: `counts`: every block holds at least 16 live particles, and some block of every draw holds exactly 64. `cell_flags`: cell kinds: 0 air, 1 fluid, 2 solid. `destination`: only live particles move. From one box, between 64 and 256 particles move in each direction, and in every box exactly 256 move in some direction. `dest_slot`: particles of one box that move in one direction have distinct slots; for staying particles the value is meaningless.
All inputs are finite; a program needn't handle non-finite values.
Results may differ from a plain program's by a relative error of at most 0.0003.
Values sent between devices are 32-bit elements; how exact they have to be, the bound alone decides.
A program may use at most 64 MiB of HBM per device.

v0:
```python
import functools

import jax
import jax.numpy as jnp
from jax import lax
from jax.experimental import pallas as pl
from jax.experimental.pallas import tpu as pltpu
from jax.sharding import PartitionSpec as P

F32, BF16, I32 = jnp.float32, jnp.bfloat16, jnp.int32
MESH = pl.DeviceIdType.MESH
STEPS = ((1, 0), (-1, 0), (0, 1), (0, -1), (1, 1), (1, -1), (-1, 1), (-1, -1))
TIME_STEP = 0.25
GRAVITY = 1.0
MASS_FLOOR = 0.5
ITERS = 4

WIDE_X = 19
FIELD_PARTS = (
    ((8, 13), (0, 5), 1),
    ((5, 11), (13, 19), 1),
    ((5, 13), (5, 13), 0),
    ((5, 13), (5, 13), 2),
    ((9, 13), (1, 5), 0),
    ((8, 13), (0, 5), 2),
    ((5, 10), (13, 18), 0),
    ((5, 11), (13, 19), 2),
)
SOURCE_PARTS = (
    ((9, 13), (1, 5), 1),
    ((5, 10), (13, 18), 1),
    ((5, 13), (5, 13), 0),
    ((5, 13), (5, 13), 2),
    ((10, 13), (2, 5), 0),
    ((9, 13), (1, 5), 2),
    ((5, 9), (13, 17), 0),
    ((5, 10), (13, 18), 2),
)
SUM_TILES = (9, 5, 9, 5, 2, 1, 1, 1)


def iota(shape, dim):
    return lax.broadcasted_iota(I32, shape, dim)


def below_z(v):
    axis = v.ndim - 1
    return jnp.where(iota(v.shape, axis) == 0, 0.0, pltpu.roll(v, 1, axis))


def above_z(v):
    axis = v.ndim - 1
    return jnp.where(iota(v.shape, axis) == 127, 0.0, pltpu.roll(v, 127, axis))


def two_parts(v):
    high = v.astype(BF16)
    return high, (v - high.astype(F32)).astype(BF16)


def dot_last(a, b):
    return lax.dot_general(a, b, (((1,), (1,)), ((), ())), preferred_element_type=F32)


def blocks_exchanged(parts):
    parts = list(parts)
    group = iota(parts[0].shape, 1) >> 3
    for bit in (1, 2, 4, 8):
        upper = (group & bit) != 0
        for i in range(16):
            if i & bit:
                continue
            low, high = parts[i], parts[i | bit]
            parts[i] = jnp.where(upper, pltpu.roll(high, 8 * bit, 1), low)
            parts[i | bit] = jnp.where(upper, high, pltpu.roll(low, 128 - 8 * bit, 1))
    return parts


def cell_row(x, y, ox, oy, k):
    return ((x + 1) * 10 + (y + 1)) * 16 + 8 * ox + 4 * oy + k


def kernel(
    nx,
    ny,
    off_h,
    vel_h,
    aff_h,
    cell_h,
    count_h,
    flag_h,
    press_h,
    dest_h,
    slot_h,
    off_o,
    vel_o,
    aff_o,
    press_o,
    rec_o,
    off_v,
    vel_v,
    aff_v,
    cell_v,
    count_v,
    dest_v,
    slot_v,
    flag_w,
    old_w,
    alive_v,
    bin_v,
    quant,
    binned,
    cells,
    nodes,
    column8,
    message0,
    message1,
    message2,
    message3,
    message4,
    message_d2,
    arrive0,
    arrive1,
    arrive2,
    arrive3,
    arrive4,
    arrive5,
    arrive6,
    arrive7,
    speed_w,
    source_w,
    scale_w,
    solid_w,
    press_a,
    press_b,
    settled,
    slot_onehot,
    parcels,
    records,
    outgoing,
    incoming,
    load_sem,
    send_sem,
    recv_sem,
):
    gx, gy = lax.axis_index("gx"), lax.axis_index("gy")
    where_x = {0: gx, 1: lax.rem(gx + 1, nx), -1: lax.rem(gx + nx - 1, nx)}
    where_y = {0: gy, 1: lax.rem(gy + 1, ny), -1: lax.rem(gy + ny - 1, ny)}
    inside_x = {0: gx >= 0, 1: gx < nx - 1, -1: gx > 0}
    inside_y = {0: gy >= 0, 1: gy < ny - 1, -1: gy > 0}

    def copy_to(number, stage, src, dst):
        dx, dy = STEPS[number]
        return pltpu.make_async_remote_copy(
            src_ref=src,
            dst_ref=dst,
            send_sem=send_sem.at[8 * stage + number],
            recv_sem=recv_sem.at[8 * stage + number],
            device_id=(where_x[dx], where_y[dy]),
            device_id_type=MESH,
        )

    own = (pl.ds(5, 8), pl.ds(8, 8))
    loads = [
        pltpu.make_async_copy(src, dst, load_sem.at[i])
        for i, (src, dst) in enumerate(
            (
                (flag_h, flag_w.at[own]),
                (press_h, old_w.at[own]),
                (count_h, count_v),
                (cell_h, cell_v),
                (off_h, off_v),
                (vel_h, vel_v),
                (aff_h, aff_v),
                (slot_h, slot_v),
                (dest_h, dest_v),
            )
        )
    ]
    for load in loads:
        load.start()

    barrier = pltpu.get_barrier_semaphore()
    for dx, dy in STEPS:
        pl.semaphore_signal(
            barrier, inc=1, device_id=(where_x[dx], where_y[dy]), device_id_type=MESH
        )

    zero_tile = jnp.zeros((8, 128), F32)
    for x in (0, 18):
        flag_w[x, 0:8] = jnp.zeros((8, 128), I32)
        old_w[x, 0:8] = zero_tile
    for x in range(WIDE_X):
        for field in (solid_w, press_a, press_b):
            field[x, 0:8] = zero_tile
            field[x, 32:40] = zero_tile
    for x in range(8):
        for half in (0, 8):
            cells[pl.ds(cell_row(x, -1, 0, 0, 0) + half, 8), :] = zero_tile
    for half in (0, 8):
        cells[pl.ds(cell_row(-1, 7, 0, 0, 0) + half, 8), :] = zero_tile

    pl.semaphore_wait(barrier, 8)
    loads[0].wait()
    loads[1].wait()

    exchanges = []
    for number in range(8):
        (s0, s1), (t0, t1), tile = FIELD_PARTS[number]
        for stage, field in ((0, flag_w), (1, old_w)):
            exchanges.append(
                copy_to(
                    number,
                    stage,
                    field.at[pl.ds(s0, s1 - s0), pl.ds(8, 8)],
                    field.at[pl.ds(t0, t1 - t0), pl.ds(8 * tile, 8)],
                )
            )
    for copy in exchanges:
        copy.start()

    for load in loads[2:7]:
        load.wait()

    sub32 = iota((32, 128), 0)
    lane32 = iota((32, 128), 1)
    for xb in range(2):
        r0 = 32 * xb
        row = iota((32, 32), 0)
        column = iota((32, 32), 1)
        totals = count_v[xb].astype(F32)
        spread = jnp.where(
            (row & 1) == 0,
            jnp.broadcast_to(totals[0:1], (32, 32)),
            jnp.broadcast_to(totals[1:2], (32, 32)),
        )
        spread = jnp.where((column >> 1) == (row >> 1), spread, 0.0).astype(BF16)
        half = ((sub32 & 1) == (lane32 >> 6)).astype(F32).astype(BF16)
        live = jnp.dot(spread, half, preferred_element_type=F32)
        alive_v[pl.ds(r0, 32), :] = jnp.where(
            (lane32 & 63).astype(F32) < live, 1.0, 0.0
        )
        number_in_block = cell_v[pl.ds(r0, 32), :]
        bin_v[pl.ds(r0, 32), :] = (
            ((number_in_block >> 2) << 3) + ((lane32 >> 6) << 2) + (number_in_block & 3)
        )

    def deposit(step, carry):
        rows = pl.ds(pl.multiple_of(step * 16, 16), 16)
        alive = alive_v[rows, :]
        f = [off_v[d, rows, :] for d in range(3)]
        a = [aff_v[j, rows, :] for j in range(9)]
        base = [
            vel_v[k, rows, :] - (a[3 * k] * f[0] + a[3 * k + 1] * f[1] + a[3 * k + 2] * f[2])
            for k in range(3)
        ]
        hx = [(1.0 - f[0]) * alive, f[0] * alive]
        hy = [1.0 - f[1], f[1]]
        hz = [1.0 - f[2], f[2]]
        for ox in range(2):
            bx = [base[k] + a[3 * k] if ox else base[k] for k in range(3)]
            for oy in range(2):
                by = [bx[k] + a[3 * k + 1] if oy else bx[k] for k in range(3)]
                hxy = hx[ox] * hy[oy]
                for oz in range(2):
                    w = hxy * hz[oz]
                    channel = 16 * oz + 8 * ox + 4 * oy
                    start = pl.multiple_of(channel * 64 + step * 16, 16)
                    quant[pl.ds(start, 16), :] = w
                    for k in range(3):
                        bz = by[k] + a[3 * k + 2] if oz else by[k]
                        start = pl.multiple_of((channel + k + 1) * 64 + step * 16, 16)
                        quant[pl.ds(start, 16), :] = w * bz
        return carry

    lax.fori_loop(0, 4, deposit, 0)

    def bin_column(col, carry):
        xb, yb = col // 2, lax.rem(col, 2)
        for zt in range(16):
            r = 32 * xb + yb + 2 * zt
            values = quant[pl.ds(r, 32, stride=64), :]
            high, low = two_parts(values)
            onehot = (
                (iota((128, 128), 0) == bin_v[pl.ds(r, 1), :]).astype(F32).astype(BF16)
            )
            total = dot_last(jnp.concatenate([high, low], axis=0), onehot)
            binned[zt] = total[0:32] + total[32:64]
        for g in range(2):
            lower = blocks_exchanged([binned[zt, 8 * g : 8 * g + 8] for zt in range(16)])
            upper = blocks_exchanged(
                [binned[zt, 16 + 8 * g : 24 + 8 * g] for zt in range(16)]
            )
            for q in range(16):
                start = ((4 * xb + q // 4 + 1) * 10 + 4 * yb + q % 4 + 1) * 16 + 8 * g
                cells[pl.ds(pl.multiple_of(start, 8), 8), :] = lower[q] + below_z(upper[q])
        return carry

    lax.fori_loop(0, 4, bin_column, 0)

    for k in range(4):
        for x in range(9):
            total = None
            for ox in range(2):
                if not 0 <= x - ox < 8:
                    continue
                for oy in range(2):
                    part = cells[pl.ds(cell_row(x - ox, -oy, ox, oy, k), 8, stride=16), :]
                    total = part if total is None else total + part
            nodes[pl.ds((k * 9 + x) * 8, 8), :] = total
        column8[k] = (
            cells[pl.ds(cell_row(0, 7, 0, 1, k), 8, stride=160), :]
            + cells[pl.ds(cell_row(-1, 7, 1, 1, k), 8, stride=160), :]
        )

    def four(x, y, ox, oy):
        return cells[pl.ds(cell_row(x, y, ox, oy, 0), 4), :]

    corner88 = four(7, 7, 1, 1)
    d1 = jnp.concatenate([corner88, four(0, 7, 0, 1)], axis=0)
    d2 = jnp.concatenate([four(7, 0, 1, 0), four(0, 0, 0, 0)], axis=0)
    d3 = jnp.concatenate(
        [four(7, 7, 0, 1) + four(6, 7, 1, 1), four(7, 7, 1, 0) + four(7, 6, 1, 1)], axis=0
    )
    for k in range(4):
        message0[2 * k] = nodes[pl.ds((k * 9 + 7) * 8, 8), :]
        message0[2 * k + 1] = nodes[pl.ds((k * 9 + 8) * 8, 8), :]
        message1[k] = nodes[pl.ds(k * 72, 8), :]
        message2[2 * k] = nodes[pl.ds(k * 72 + 7, 8, stride=8), :]
        message2[2 * k + 1] = column8[k]
        message3[k] = nodes[pl.ds(k * 72, 8, stride=8), :]
    message0[8] = d1
    message1[4] = d1
    message2[8] = d1
    message3[4] = d2
    message4[0] = d1
    message4[1] = d3
    message_d2[0] = d2

    sums = [
        copy_to(number, 2, src, dst)
        for number, src, dst in (
            (0, message0, arrive0),
            (1, message1, arrive1),
            (2, message2, arrive2),
            (3, message3, arrive3),
            (4, message4, arrive4),
            (5, message_d2, arrive5),
            (6, message4.at[pl.ds(0, 1)], arrive6),
            (7, message_d2, arrive7),
        )
    ]
    for copy in sums:
        copy.start()

    loads[7].wait()
    loads[8].wait()

    def slot_rows(step, carry):
        for j in range(4):
            r = 4 * step + j
            slot = jnp.where(dest_v[pl.ds(r, 1), :] > 0, slot_v[pl.ds(r, 1), :], -1)
            slot_onehot[:, pl.ds(pl.multiple_of(r * 128, 128), 128)] = (
                (iota((256, 128), 0) == slot).astype(F32).astype(BF16)
            )
        return carry

    for copy in exchanges:
        copy.wait_recv()

    sub24 = iota((24, 128), 0)
    ok_y = jnp.where(
        sub24 < 8,
        inside_y[-1].astype(I32),
        jnp.where(sub24 >= 16, inside_y[1].astype(I32), 1),
    )
    for x in range(WIDE_X):
        side = -1 if x < 5 else 1 if x >= 13 else 0
        kind = flag_w[x]
        kind = kind * ok_y
        if side:
            kind = kind * inside_x[side].astype(I32)
        solid_w[x, 8:32] = jnp.where(kind == 2, 1.0, 0.0)
        fluid = kind == 1
        scale_w[x] = jnp.where(fluid, 1.0, 0.0)
        press_a[x, 8:32] = jnp.where(fluid, old_w[x], 0.0)
    for x in range(1, WIDE_X - 1):
        middle = solid_w[x, 8:32]
        closed = (
            solid_w[x - 1, 8:32]
            + solid_w[x + 1, 8:32]
            + solid_w[x, 7:31]
            + solid_w[x, 9:33]
            + below_z(middle)
            + above_z(middle)
        )
        scale_w[x] = scale_w[x] / jnp.maximum(6.0 - closed, 1.0)

    lax.fori_loop(0, 8, slot_rows, 0)

    for copy in sums:
        copy.wait_recv()

    sub8 = iota((8, 128), 0)

    def kept(v, dx, dy):
        if dx:
            v = jnp.where(inside_x[dx], v, 0.0)
        if dy:
            v = jnp.where(inside_y[dy], v, 0.0)
        return v

    def at_first(v, row):
        return jnp.where(sub8 == 0, v + row, v)

    speed_f = speed_w.reshape(3 * 10 * 24, 128)
    flag_f = flag_w.reshape(WIDE_X * 24, 128)

    def normalised(sums4, kind, dx, dy):
        inverse = 1.0 / jnp.maximum(sums4[0], MASS_FLOOR)
        result = []
        for k in range(3):
            u = sums4[k + 1] * inverse
            if k == 2:
                u = u - TIME_STEP * GRAVITY
            result.append(kept(jnp.where(kind == 2, 0.0, u), dx, dy))
        return result

    minus_rows, zero_rows, plus_rows, below_columns, upper_columns = [], [], [], [], []
    for k in range(4):
        minus_rows.append(
            at_first(
                kept(arrive0[2 * k], -1, 0), kept(arrive4[1, k : k + 1], -1, -1)
            )
        )
        first = nodes[pl.ds(k * 72, 8), :] + kept(arrive0[2 * k + 1], -1, 0)
        nodes[pl.ds(k * 72, 8), :] = first
        column = at_first(
            kept(arrive2[2 * k + 1], 0, -1), kept(arrive4[0, k : k + 1], -1, -1)
        )
        nodes[pl.ds(k * 72, 8, stride=8), :] = (
            nodes[pl.ds(k * 72, 8, stride=8), :] + column
        )
        plus_rows.append(
            at_first(
                nodes[pl.ds((k * 9 + 8) * 8, 8), :] + kept(arrive1[k], 1, 0),
                kept(arrive2[8, k : k + 1], 0, -1)
                + kept(arrive6[0, 4 + k : 5 + k], 1, -1),
            )
        )
        below_columns.append(
            at_first(
                kept(arrive2[2 * k], 0, -1), kept(arrive4[1, 4 + k : 5 + k], -1, -1)
            )
        )
        upper_columns.append(
            at_first(
                column8[k] + kept(arrive3[k], 0, 1),
                kept(arrive0[8, k : k + 1], -1, 0) + kept(arrive5[0, k : k + 1], -1, 1),
            )
        )
    corner = (
        message4[0, 0:4]
        + kept(arrive1[4, 4:8], 1, 0)
        + kept(arrive3[4, 0:4], 0, 1)
        + kept(arrive7[0, 4:8], 1, 1)
    )

    for x in range(-1, 9):
        if x == -1:
            sums4, side = minus_rows, -1
        elif x == 8:
            sums4, side = plus_rows, 1
        else:
            sums4 = [nodes[pl.ds((k * 9 + x) * 8, 8), :] for k in range(4)]
            side = 0
        u = normalised(sums4, flag_w[x + 5, 8:16], side, 0)
        for k in range(3):
            speed_w[k, x + 1, 8:16] = u[k]
    for columns, y, side in ((below_columns, 7, -1), (upper_columns, 16, 1)):
        u = normalised(columns, flag_f[pl.ds(5 * 24 + y, 8, stride=24), :], 0, side)
        for k in range(3):
            speed_f[pl.ds((k * 10 + 1) * 24 + y, 8, stride=24), :] = u[k]
    u = normalised(
        [corner[k : k + 1] for k in range(4)], flag_w[13, 16:17], 1, 1
    )
    for k in range(3):
        speed_w[k, 9, 16:17] = u[k]

    for x in range(8):
        source_w[x + 5, 8:16] = 0.5 * (
            speed_w[0, x + 2, 8:16]
            - speed_w[0, x, 8:16]
            + (speed_w[1, x + 1, 9:17] - speed_w[1, x + 1, 7:15])
            + (above_z(speed_w[2, x + 1, 8:16]) - below_z(speed_w[2, x + 1, 8:16]))
        )

    margins = []
    for number in range(8):
        (s0, s1), (t0, t1), tile = SOURCE_PARTS[number]
        margins.append(
            copy_to(
                number,
                3,
                source_w.at[pl.ds(s0, s1 - s0), pl.ds(8, 8)],
                source_w.at[pl.ds(t0, t1 - t0), pl.ds(8 * tile, 8)],
            )
        )
    for copy in margins:
        copy.start()
    lax.fori_loop(8, 16, slot_rows, 0)
    for copy in margins:
        copy.wait_recv()

    old, new = press_a, press_b
    for sweep in range(ITERS):
        low, high = sweep + 1, WIDE_X - 1 - sweep
        for x in range(low, high):
            middle = old[x, 8:32]
            near = (
                old[x - 1, 8:32]
                + old[x + 1, 8:32]
                + old[x, 7:31]
                + old[x, 9:33]
                + below_z(middle)
                + above_z(middle)
            )
            scale = scale_w[x]
            new[x, 8:32] = jnp.where(scale > 0.0, scale * (near - source_w[x]), 0.0)
        old, new = new, old
    for x in range(8):
        press_o[x] = old[x + 5, 16:24]

    for x in range(9):
        w = x + 5
        p, s = old[w, 16:32], solid_w[w, 16:32]
        fluid = scale_w[w, 8:24] > 0.0
        slopes = (
            old[w + 1, 16:32]
            - old[w - 1, 16:32]
            + p * (solid_w[w + 1, 16:32] - solid_w[w - 1, 16:32]),
            old[w, 17:33]
            - old[w, 15:31]
            + p * (solid_w[w, 17:33] - solid_w[w, 15:31]),
            above_z(p) - below_z(p) + p * (above_z(s) - below_z(s)),
        )
        for k in range(3):
            settled[k, x] = speed_w[k, x + 1, 8:24] - jnp.where(fluid, 0.5 * slopes[k], 0.0)

    odd8 = (iota((8, 128), 0) & 1) == 1
    for xb in range(2):
        rows = pl.ds(32 * xb, 32)
        cell = cell_v[rows, :]
        alive = alive_v[rows, :]
        qx, qy = cell >> 4, (cell >> 2) & 3
        z = ((sub32 >> 1) << 3) + ((lane32 >> 6) << 2) + (cell & 3)
        f = [off_v[d, rows, :] for d in range(3)]
        speeds, offsets = [], []
        for k in range(3):
            pick_x = [[None] * 4, [None] * 4]
            for ix in range(5):
                pick_y = [[None] * 2, [None] * 2]
                for iy in range(5):
                    even = jnp.broadcast_to(settled[k, 4 * xb + ix, iy : iy + 1], (8, 128))
                    odd = jnp.broadcast_to(settled[k, 4 * xb + ix, iy + 4 : iy + 5], (8, 128))
                    table = jnp.where(odd8, odd, even)
                    rise = above_z(table) - table
                    got = [
                        jnp.take_along_axis(jnp.concatenate([t] * 4, axis=0), z, axis=1)
                        for t in (table, rise)
                    ]
                    for o in range(2):
                        if not 0 <= iy - o < 4:
                            continue
                        for j in range(2):
                            held = pick_y[o][j]
                            pick_y[o][j] = (
                                got[j]
                                if held is None
                                else jnp.where(qy == iy - o, got[j], held)
                            )
                flat = pick_y[0] + pick_y[1]
                for o in range(2):
                    if not 0 <= ix - o < 4:
                        continue
                    for j in range(4):
                        held = pick_x[o][j]
                        pick_x[o][j] = (
                            flat[j] if held is None else jnp.where(qx == ix - o, flat[j], held)
                        )
            value, along_y, along_z = [], [], []
            for o in range(2):
                a0, d0, a1, d1_ = pick_x[o]
                v0 = a0 + f[2] * d0
                v1 = a1 + f[2] * d1_
                along_y.append(v1 - v0)
                value.append(v0 + f[1] * (v1 - v0))
                along_z.append(d0 + f[1] * (d1_ - d0))
            along_x = value[1] - value[0]
            speed = (value[0] + f[0] * along_x) * alive
            offset = f[k] + TIME_STEP * speed
            speeds.append(speed)
            offsets.append(offset)
            slope = (
                along_x * alive,
                (along_y[0] + f[0] * (along_y[1] - along_y[0])) * alive,
                (along_z[0] + f[0] * (along_z[1] - along_z[0])) * alive,
            )
            off_o[k, rows, :] = offset
            vel_o[k, rows, :] = speed
            records[pl.ds((3 + k) * 64 + 32 * xb, 32), :] = speed
            for b in range(3):
                aff_o[3 * k + b, rows, :] = slope[b]
                records[pl.ds((6 + 3 * k + b) * 64 + 32 * xb, 32), :] = slope[b]
        moving = dest_v[rows, :]

        def one_of(*numbers):
            hit = moving == numbers[0]
            for number in numbers[1:]:
                hit = hit | (moving == number)
            return jnp.where(hit, 8, 0)

        place = (
            4 * xb + qx - one_of(1, 5, 6) + one_of(2, 7, 8),
            None,
            z,
        )
        row_y = (sub32 & 1) << 2
        place = (
            place[0],
            row_y + qy - one_of(3, 5, 7) + one_of(4, 6, 8),
            z,
        )
        for d in range(3):
            records[pl.ds(d * 64 + 32 * xb, 32), :] = place[d].astype(F32) + offsets[d]
        records[pl.ds(15 * 64 + 32 * xb, 32), :] = jnp.zeros((32, 128), F32)

    def parcel_rows(step, carry):
        for j in range(4):
            r = 4 * step + j
            record = records[pl.ds(r, 16, stride=64), :]
            high, low = two_parts(record)
            moving = jnp.broadcast_to(dest_v[pl.ds(r, 1), :], (16, 128))
            lanes = pl.ds(pl.multiple_of(r * 128, 128), 128)
            for number in range(8):
                picked = (moving == number + 1).astype(F32).astype(BF16)
                parcels[pl.ds(32 * number, 16), lanes] = high * picked
                parcels[pl.ds(32 * number + 16, 16), lanes] = low * picked
        return carry

    lax.fori_loop(0, 16, parcel_rows, 0)
    leaving = [None] * 8
    for half in (1, 0):
        placed = dot_last(parcels[pl.ds(128 * half, 128), :], slot_onehot[...])
        for j in range(4):
            number = 4 * half + j
            outgoing[number] = placed[32 * j : 32 * j + 16] + placed[32 * j + 16 : 32 * j + 32]
            leaving[number] = copy_to(number, 4, outgoing.at[number], incoming.at[number])
            leaving[number].start()

    for copy in exchanges + sums + margins:
        copy.wait_send()

    rec_f = rec_o.reshape(15 * 16, 128)
    for number in (4, 5, 6, 7, 0, 1, 2, 3):
        leaving[number].wait()
        dx, dy = STEPS[number]
        arrived = kept(incoming[number], -dx, -dy)
        for half in range(2):
            rec_f[pl.ds(2 * number + half, 15, stride=16), :] = arrived[
                0:15, 128 * half : 128 * half + 128
            ]


def in_rows(a):
    lead = a.shape[:-3]
    n = len(lead)
    turned = a.reshape(lead + (2, 2, 16, 128)).transpose(
        tuple(range(n)) + (n, n + 2, n + 1, n + 3)
    )
    return turned.reshape(lead + (64, 128))


def from_rows(a):
    lead = a.shape[:-2]
    n = len(lead)
    turned = a.reshape(lead + (2, 16, 2, 128)).transpose(
        tuple(range(n)) + (n, n + 2, n + 1, n + 3)
    )
    return turned.reshape(lead + (2, 2, 2048))


def on_device(
    nx,
    ny,
    cell_offset,
    velocity,
    affine,
    cell_index,
    counts,
    cell_flags,
    old_pressure,
    destination,
    dest_slot,
):
    vmem = pl.BlockSpec(memory_space=pltpu.VMEM)
    anywhere = pl.BlockSpec(memory_space=pltpu.HBM)

    def f32(*shape):
        return pltpu.VMEM(shape, F32)

    outs = pl.pallas_call(
        functools.partial(kernel, nx, ny),
        out_shape=[
            jax.ShapeDtypeStruct((3, 64, 128), F32),
            jax.ShapeDtypeStruct((3, 64, 128), F32),
            jax.ShapeDtypeStruct((9, 64, 128), F32),
            jax.ShapeDtypeStruct((8, 8, 128), F32),
            jax.ShapeDtypeStruct((15, 16, 128), F32),
        ],
        in_specs=[anywhere] * 9,
        out_specs=[vmem] * 5,
        scratch_shapes=[
            f32(3, 64, 128),
            f32(3, 64, 128),
            f32(9, 64, 128),
            pltpu.VMEM((64, 128), I32),
            pltpu.VMEM((2, 2, 32), I32),
            pltpu.VMEM((64, 128), I32),
            pltpu.VMEM((64, 128), I32),
            pltpu.VMEM((WIDE_X, 24, 128), I32),
            f32(WIDE_X, 24, 128),
            f32(64, 128),
            pltpu.VMEM((64, 128), I32),
            f32(32 * 64, 128),
            f32(16, 32, 128),
            f32(10 * 10 * 16, 128),
            f32(4 * 9 * 8, 128),
            f32(4, 8, 128),
            f32(9, 8, 128),
            f32(5, 8, 128),
            f32(9, 8, 128),
            f32(5, 8, 128),
            f32(2, 8, 128),
            f32(1, 8, 128),
        ]
        + [f32(tiles, 8, 128) for tiles in SUM_TILES]
        + [
            f32(3, 10, 24, 128),
            f32(WIDE_X, 24, 128),
            f32(WIDE_X, 24, 128),
            f32(WIDE_X, 40, 128),
            f32(WIDE_X, 40, 128),
            f32(WIDE_X, 40, 128),
            f32(3, 9, 16, 128),
            pltpu.VMEM((256, 8192), BF16),
            pltpu.VMEM((256, 8192), BF16),
            f32(16 * 64, 128),
            f32(8, 16, 256),
            f32(8, 16, 256),
            pltpu.SemaphoreType.DMA((9,)),
            pltpu.SemaphoreType.DMA((40,)),
            pltpu.SemaphoreType.DMA((40,)),
        ],
        compiler_params=pltpu.CompilerParams(
            collective_id=0, has_side_effects=True, vmem_limit_bytes=48 * 1024 * 1024
        ),
        name="substep",
    )(
        in_rows(cell_offset),
        in_rows(velocity),
        in_rows(affine),
        in_rows(cell_index),
        counts,
        cell_flags,
        old_pressure,
        in_rows(destination),
        in_rows(dest_slot),
    )
    return (
        from_rows(outs[0]),
        from_rows(outs[1]),
        from_rows(outs[2]),
        outs[3],
        outs[4].reshape(15, 8, 1, 256),
    )


def solution(mesh):
    particles, blocks = P(None, "gx", "gy", None), P("gx", "gy", None)
    return jax.shard_map(
        functools.partial(on_device, mesh.shape["gx"], mesh.shape["gy"]),
        mesh=mesh,
        in_specs=(particles, particles, particles) + (blocks,) * 6,
        out_specs=(particles, particles, particles, blocks, P(None, None, "gx", "gy")),
        check_vma=False,
    )
```

profile of v0, /device:TPU:1, one launch (start us, length us, event | category | flops | bytes accessed | tf_op | source)
XLA Modules:
  0.0 62.6 jit_solution(12892337341527502071)
XLA Ops:
  0.6 0.0 copy-start.8
  0.6 0.7 %copy-done.8 = s32[2,2,32]{2,1,0:T(2,128)S(1)} copy-done((s32[2,2,32]{2,1,0:T(2,128)S(1)}, s32[2,2,32]{2,1,0:T(2,128)}, u32[]{:S(2)}) %copy-start.8) | copy-done | bytes 536
  1.3 0.0 copy-start
  1.3 1.0 %copy-done = f32[9,2,2,2048]{3,2,1,0:T(2,128)S(1)} copy-done((f32[9,2,2,2048]{3,2,1,0:T(2,128)S(1)}, f32[9,2,2,2048]{3,2,1,0:T(2,128)}, u32[]{:S(2)}) %copy-start) | copy-done | bytes 294936
  2.3 0.0 copy-start.1
  2.3 0.9 %copy-done.1 = f32[3,2,2,2048]{3,2,1,0:T(2,128)S(1)} copy-done((f32[3,2,2,2048]{3,2,1,0:T(2,128)S(1)}, f32[3,2,2,2048]{3,2,1,0:T(2,128)}, u32[]{:S(2)}) %copy-start.1) | copy-done | bytes 98328
  3.2 0.0 copy-start.2
  3.2 0.9 %copy-done.2 = f32[3,2,2,2048]{3,2,1,0:T(2,128)S(1)} copy-done((f32[3,2,2,2048]{3,2,1,0:T(2,128)S(1)}, f32[3,2,2,2048]{3,2,1,0:T(2,128)}, u32[]{:S(2)}) %copy-start.2) | copy-done | bytes 98328
  4.1 0.0 copy-start.3
  4.1 0.8 %copy-done.3 = s32[2,2,2048]{2,1,0:T(2,128)S(1)} copy-done((s32[2,2,2048]{2,1,0:T(2,128)S(1)}, s32[2,2,2048]{2,1,0:T(2,128)}, u32[]{:S(2)}) %copy-start.3) | copy-done | bytes 32792
  4.8 0.0 copy-start.4
  4.8 0.8 %copy-done.4 = s32[8,8,128]{2,1,0:T(8,128)S(1)} copy-done((s32[8,8,128]{2,1,0:T(8,128)S(1)}, s32[8,8,128]{2,1,0:T(8,128)}, u32[]{:S(2)}) %copy-start.4) | copy-done | bytes 32792
  5.6 0.0 copy-start.5
  5.6 0.8 %copy-done.5 = f32[8,8,128]{2,1,0:T(8,128)S(1)} copy-done((f32[8,8,128]{2,1,0:T(8,128)S(1)}, f32[8,8,128]{2,1,0:T(8,128)}, u32[]{:S(2)}) %copy-start.5) | copy-done | bytes 32792
  6.3 0.0 copy-start.6
  6.3 0.8 %copy-done.6 = s32[2,2,2048]{2,1,0:T(2,128)S(1)} copy-done((s32[2,2,2048]{2,1,0:T(2,128)S(1)}, s32[2,2,2048]{2,1,0:T(2,128)}, u32[]{:S(2)}) %copy-start.6) | copy-done | bytes 32792
  7.1 0.0 copy-start.7
  7.1 0.8 %copy-done.7 = s32[2,2,2048]{2,1,0:T(2,128)S(1)} copy-done((s32[2,2,2048]{2,1,0:T(2,128)S(1)}, s32[2,2,2048]{2,1,0:T(2,128)}, u32[]{:S(2)}) %copy-start.7) | copy-done | bytes 32792
  7.9 51.5 %substep.1 = (f32[3,64,128]{2,1,0:T(8,128)S(1)}, f32[3,64,128]{2,1,0:T(8,128)S(1)}, f32[9,64,128]{2,1,0:T(8,128)S(1)}, f32[8,8,128]{2,1,0:T(8,128)S(1)}, f32[15,16,128]{2,1,0:T(8,128)S(1)}) custom-call(f32[3,64,128]{2,1,0:T(8,128)S(1)} %bitcast.49, f32[3,64,128]{2,1,0:T(8,128)S(1)} %bitcast.50, f32[9,64,128]{2,1,0:T(8,128)S(1)} %bitcast.46, ...), custom_call_target="tpu_custom_call" | custom-call | tf_op jit(solution)/shard_map/substep/pallas_call | solution.py:712
  59.3 0.6 %copy.29 = f32[3,2,2,2048]{3,2,1,0:T(2,128)} copy(f32[3,2,2,2048]{3,2,1,0:T(2,128)S(1)} %bitcast.52) | data formatting | bytes 196608
  60.0 0.6 %copy.30 = f32[3,2,2,2048]{3,2,1,0:T(2,128)} copy(f32[3,2,2,2048]{3,2,1,0:T(2,128)S(1)} %bitcast.51) | data formatting | bytes 196608
  60.6 0.7 %copy.31 = f32[9,2,2,2048]{3,2,1,0:T(2,128)} copy(f32[9,2,2,2048]{3,2,1,0:T(2,128)S(1)} %bitcast.47) | data formatting | bytes 589824
  61.3 0.6 copy.32
  61.9 0.6 %copy.33 = f32[15,8,1,256]{3,2,1,0:T(1,128)} copy(f32[15,8,1,256]{3,2,1,0:T(1,128)S(1)} %bitcast.48) | data formatting | bytes 245760
Async XLA Ops:
  0.6 0.7 %copy-start.8 = (s32[2,2,32]{2,1,0:T(2,128)S(1)}, s32[2,2,32]{2,1,0:T(2,128)}, u32[]{:S(2)}) copy-start(s32[2,2,32]{2,1,0:T(2,128)} %count_h.1) | copy-start | bytes 1540
  1.3 1.0 %copy-start = (f32[9,2,2,2048]{3,2,1,0:T(2,128)S(1)}, f32[9,2,2,2048]{3,2,1,0:T(2,128)}, u32[]{:S(2)}) copy-start(f32[9,2,2,2048]{3,2,1,0:T(2,128)} %param.11) | copy-start | bytes 884740
  2.3 0.9 %copy-start.1 = (f32[3,2,2,2048]{3,2,1,0:T(2,128)S(1)}, f32[3,2,2,2048]{3,2,1,0:T(2,128)}, u32[]{:S(2)}) copy-start(f32[3,2,2,2048]{3,2,1,0:T(2,128)} %param.9) | copy-start | bytes 294916
  3.2 0.9 %copy-start.2 = (f32[3,2,2,2048]{3,2,1,0:T(2,128)S(1)}, f32[3,2,2,2048]{3,2,1,0:T(2,128)}, u32[]{:S(2)}) copy-start(f32[3,2,2,2048]{3,2,1,0:T(2,128)} %param.10) | copy-start | bytes 294916
  4.1 0.8 %copy-start.3 = (s32[2,2,2048]{2,1,0:T(2,128)S(1)}, s32[2,2,2048]{2,1,0:T(2,128)}, u32[]{:S(2)}) copy-start(s32[2,2,2048]{2,1,0:T(2,128)} %param.12) | copy-start | bytes 98308
  4.8 0.8 %copy-start.4 = (s32[8,8,128]{2,1,0:T(8,128)S(1)}, s32[8,8,128]{2,1,0:T(8,128)}, u32[]{:S(2)}) copy-start(s32[8,8,128]{2,1,0:T(8,128)} %flag_h.1) | copy-start | bytes 98308
  5.6 0.8 %copy-start.5 = (f32[8,8,128]{2,1,0:T(8,128)S(1)}, f32[8,8,128]{2,1,0:T(8,128)}, u32[]{:S(2)}) copy-start(f32[8,8,128]{2,1,0:T(8,128)} %press_h.1) | copy-start | bytes 98308
  6.3 0.8 %copy-start.6 = (s32[2,2,2048]{2,1,0:T(2,128)S(1)}, s32[2,2,2048]{2,1,0:T(2,128)}, u32[]{:S(2)}) copy-start(s32[2,2,2048]{2,1,0:T(2,128)} %param.16) | copy-start | bytes 98308
  7.1 0.8 %copy-start.7 = (s32[2,2,2048]{2,1,0:T(2,128)S(1)}, s32[2,2,2048]{2,1,0:T(2,128)}, u32[]{:S(2)}) copy-start(s32[2,2,2048]{2,1,0:T(2,128)} %param.17) | copy-start | bytes 98308
where the time goes:
time: 63.2 us; the launch traced here: 62.6 us
  Pallas kernels  51.5 us (81%)
  local copies, waits for them, and re-layouts  10.5 us (17%)
  between operations  0.66 us (1%)
    pallas_call x1, Pallas kernels, on_device(): pl.pallas_call(functools.partial(kernel, nx, ny), out_shape=[jax.ShapeDty...  51.5 us
    unnamed x23, local copies, waits for them, and re-layouts  10.5 us

commit v1 on v0

--- a/solution.py
+++ b/solution.py
@@ -16,27 +16,28 @@
 ITERS = 4
 
 WIDE_X = 19
-FIELD_PARTS = (
-    ((8, 13), (0, 5), 1),
-    ((5, 11), (13, 19), 1),
-    ((5, 13), (5, 13), 0),
-    ((5, 13), (5, 13), 2),
-    ((9, 13), (1, 5), 0),
-    ((8, 13), (0, 5), 2),
-    ((5, 10), (13, 18), 0),
-    ((5, 11), (13, 19), 2),
-)
-SOURCE_PARTS = (
-    ((9, 13), (1, 5), 1),
-    ((5, 10), (13, 18), 1),
-    ((5, 13), (5, 13), 0),
-    ((5, 13), (5, 13), 2),
-    ((10, 13), (2, 5), 0),
-    ((9, 13), (1, 5), 2),
-    ((5, 9), (13, 17), 0),
-    ((5, 10), (13, 18), 2),
-)
-SUM_TILES = (9, 5, 9, 5, 2, 1, 1, 1)
+FIELD_REACH = ITERS + 1
+SOURCE_REACH = ITERS
+
+
+def corner_runs(number, reach):
+    dx, dy = STEPS[number]
+    runs = []
+    for far in range(1, reach + 1) if dx > 0 else range(reach + 1):
+        x = 8 - far if dx > 0 else far
+        left = reach - far
+        if dy > 0 and left > 0:
+            runs.append((x, 8 - left, x - 8 * dx, -left, left))
+        elif dy < 0:
+            runs.append((x, 0, x - 8 * dx, 8, left + 1))
+    return runs
+
+
+def corner_tiles(number, reach):
+    return -(-sum(run[4] for run in corner_runs(number, reach)) // 8)
+
+
+SUM_TILES = (7, 5, 7, 5, 2, 1, 1, 1)
 
 
 def iota(shape, dim):
@@ -56,6 +57,12 @@
 def two_parts(v):
     high = v.astype(BF16)
     return high, (v - high.astype(F32)).astype(BF16)
+
+
+def matches(row, count):
+    places = iota((count, 128), 0).astype(F32).astype(BF16)
+    wanted = jnp.broadcast_to(row.astype(F32), (count, 128)).astype(BF16)
+    return jnp.where(places == wanted, 1.0, 0.0).astype(BF16)
 
 
 def dot_last(a, b):
@@ -104,8 +111,8 @@
     count_v,
     dest_v,
     slot_v,
-    flag_w,
-    old_w,
+    flag_v,
+    field_w,
     alive_v,
     bin_v,
     quant,
@@ -127,6 +134,10 @@
     arrive5,
     arrive6,
     arrive7,
+    field_out,
+    field_in,
+    source_out,
+    source_in,
     speed_w,
     source_w,
     scale_w,
@@ -134,6 +145,7 @@
     press_a,
     press_b,
     settled,
+    tables,
     slot_onehot,
     parcels,
     records,
@@ -160,13 +172,72 @@
             device_id_type=MESH,
         )
 
-    own = (pl.ds(5, 8), pl.ds(8, 8))
+    def flat_rows(field):
+        return field.reshape(field.shape[0] * WIDE_X * 24, 128)
+
+    def halo(stage, field, outs, ins, reach):
+        flat = flat_rows(field)
+        lows, highs = reach, reach + 1
+        copies = [
+            copy_to(
+                0,
+                stage,
+                field.at[:, pl.ds(13 - lows, lows), pl.ds(8, 8)],
+                field.at[:, pl.ds(5 - lows, lows), pl.ds(8, 8)],
+            ),
+            copy_to(
+                1,
+                stage,
+                field.at[:, pl.ds(5, highs), pl.ds(8, 8)],
+                field.at[:, pl.ds(13, highs), pl.ds(8, 8)],
+            ),
+        ]
+        for number in range(2, 8):
+            out = outs[number - 2]
+            for c in range(field.shape[0]):
+                if number < 4:
+                    first, columns = (8 - lows, lows) if number == 2 else (0, highs)
+                    for j in range(columns):
+                        start = (c * WIDE_X + 5) * 24 + 8 + first + j
+                        out[c, pl.ds(8 * j, 8)] = flat[pl.ds(start, 8, stride=24), :]
+                else:
+                    row = 0
+                    for x, y, _, _, length in corner_runs(number, reach):
+                        out[c, row : row + length] = field[c, x + 5, y + 8 : y + 8 + length]
+                        row += length
+            copies.append(copy_to(number, stage, out, ins[number - 2]))
+        return copies
+
+    def unpack(field, ins, reach):
+        flat = flat_rows(field)
+        for number in range(2, 8):
+            got = ins[number - 2]
+            for c in range(field.shape[0]):
+                if number < 4:
+                    first, columns = (8 - reach, reach) if number == 2 else (16, reach + 1)
+                    for j in range(columns):
+                        start = (c * WIDE_X + 5) * 24 + first + j
+                        flat[pl.ds(start, 8, stride=24), :] = got[c, pl.ds(8 * j, 8)]
+                else:
+                    row = 0
+                    for _, _, x, y, length in corner_runs(number, reach):
+                        field[c, x + 5, y + 8 : y + 8 + length] = got[c, row : row + length]
+                        row += length
+
+    def kept(v, dx, dy):
+        if dx:
+            v = jnp.where(inside_x[dx], v, 0.0)
+        if dy:
+            v = jnp.where(inside_y[dy], v, 0.0)
+        return v
+
+    own = (1, pl.ds(5, 8), pl.ds(8, 8))
     loads = [
         pltpu.make_async_copy(src, dst, load_sem.at[i])
         for i, (src, dst) in enumerate(
             (
-                (flag_h, flag_w.at[own]),
-                (press_h, old_w.at[own]),
+                (flag_h, flag_v),
+                (press_h, field_w.at[own]),
                 (count_h, count_v),
                 (cell_h, cell_v),
                 (off_h, off_v),
@@ -187,9 +258,6 @@
         )
 
     zero_tile = jnp.zeros((8, 128), F32)
-    for x in (0, 18):
-        flag_w[x, 0:8] = jnp.zeros((8, 128), I32)
-        old_w[x, 0:8] = zero_tile
     for x in range(WIDE_X):
         for field in (solid_w, press_a, press_b):
             field[x, 0:8] = zero_tile
@@ -204,18 +272,9 @@
     loads[0].wait()
     loads[1].wait()
 
-    exchanges = []
-    for number in range(8):
-        (s0, s1), (t0, t1), tile = FIELD_PARTS[number]
-        for stage, field in ((0, flag_w), (1, old_w)):
-            exchanges.append(
-                copy_to(
-                    number,
-                    stage,
-                    field.at[pl.ds(s0, s1 - s0), pl.ds(8, 8)],
-                    field.at[pl.ds(t0, t1 - t0), pl.ds(8 * tile, 8)],
-                )
-            )
+    for x in range(8):
+        field_w[0, x + 5, 8:16] = flag_v[x].astype(F32)
+    exchanges = halo(0, field_w, field_out, field_in, FIELD_REACH)
     for copy in exchanges:
         copy.start()
 
@@ -281,19 +340,24 @@
             r = 32 * xb + yb + 2 * zt
             values = quant[pl.ds(r, 32, stride=64), :]
             high, low = two_parts(values)
-            onehot = (
-                (iota((128, 128), 0) == bin_v[pl.ds(r, 1), :]).astype(F32).astype(BF16)
-            )
+            onehot = matches(bin_v[pl.ds(r, 1), :], 128)
             total = dot_last(jnp.concatenate([high, low], axis=0), onehot)
             binned[zt] = total[0:32] + total[32:64]
+        first_z = (iota((8, 128), 1) & 7) == 0
         for g in range(2):
-            lower = blocks_exchanged([binned[zt, 8 * g : 8 * g + 8] for zt in range(16)])
-            upper = blocks_exchanged(
-                [binned[zt, 16 + 8 * g : 24 + 8 * g] for zt in range(16)]
-            )
+            parts = []
+            for zt in range(16):
+                same = pltpu.roll(binned[zt, 16 + 8 * g : 24 + 8 * g], 1, 1)
+                before = (
+                    pltpu.roll(binned[zt - 1, 16 + 8 * g : 24 + 8 * g], 121, 1) if zt else 0.0
+                )
+                parts.append(
+                    binned[zt, 8 * g : 8 * g + 8] + jnp.where(first_z, before, same)
+                )
+            parts = blocks_exchanged(parts)
             for q in range(16):
                 start = ((4 * xb + q // 4 + 1) * 10 + 4 * yb + q % 4 + 1) * 16 + 8 * g
-                cells[pl.ds(pl.multiple_of(start, 8), 8), :] = lower[q] + below_z(upper[q])
+                cells[pl.ds(pl.multiple_of(start, 8), 8), :] = parts[q]
         return carry
 
     lax.fori_loop(0, 4, bin_column, 0)
@@ -323,22 +387,24 @@
         [four(7, 7, 0, 1) + four(6, 7, 1, 1), four(7, 7, 1, 0) + four(7, 6, 1, 1)], axis=0
     )
     for k in range(4):
-        message0[2 * k] = nodes[pl.ds((k * 9 + 7) * 8, 8), :]
-        message0[2 * k + 1] = nodes[pl.ds((k * 9 + 8) * 8, 8), :]
+        message0[k] = nodes[pl.ds((k * 9 + 8) * 8, 8), :]
         message1[k] = nodes[pl.ds(k * 72, 8), :]
-        message2[2 * k] = nodes[pl.ds(k * 72 + 7, 8, stride=8), :]
-        message2[2 * k + 1] = column8[k]
+        message2[k] = column8[k]
         message3[k] = nodes[pl.ds(k * 72, 8, stride=8), :]
-    message0[8] = d1
+    for i, k in enumerate((0, 1)):
+        message0[4 + i] = nodes[pl.ds((k * 9 + 7) * 8, 8), :]
+    for i, k in enumerate((0, 2)):
+        message2[4 + i] = nodes[pl.ds(k * 72 + 7, 8, stride=8), :]
+    message0[6] = d1
     message1[4] = d1
-    message2[8] = d1
+    message2[6] = d1
     message3[4] = d2
     message4[0] = d1
     message4[1] = d3
     message_d2[0] = d2
 
     sums = [
-        copy_to(number, 2, src, dst)
+        copy_to(number, 1, src, dst)
         for number, src, dst in (
             (0, message0, arrive0),
             (1, message1, arrive1),
@@ -360,30 +426,26 @@
         for j in range(4):
             r = 4 * step + j
             slot = jnp.where(dest_v[pl.ds(r, 1), :] > 0, slot_v[pl.ds(r, 1), :], -1)
-            slot_onehot[:, pl.ds(pl.multiple_of(r * 128, 128), 128)] = (
-                (iota((256, 128), 0) == slot).astype(F32).astype(BF16)
-            )
+            lanes = pl.ds(pl.multiple_of(r * 128, 128), 128)
+            slot_onehot[:, lanes] = matches(slot, 256)
         return carry
 
     for copy in exchanges:
         copy.wait_recv()
+    unpack(field_w, field_in, FIELD_REACH)
 
     sub24 = iota((24, 128), 0)
-    ok_y = jnp.where(
-        sub24 < 8,
-        inside_y[-1].astype(I32),
-        jnp.where(sub24 >= 16, inside_y[1].astype(I32), 1),
-    )
+    ok_y = (
+        jnp.where(sub24 < 8, inside_y[-1].astype(I32), 1)
+        * jnp.where(sub24 >= 16, inside_y[1].astype(I32), 1)
+    ) > 0
     for x in range(WIDE_X):
         side = -1 if x < 5 else 1 if x >= 13 else 0
-        kind = flag_w[x]
-        kind = kind * ok_y
-        if side:
-            kind = kind * inside_x[side].astype(I32)
-        solid_w[x, 8:32] = jnp.where(kind == 2, 1.0, 0.0)
-        fluid = kind == 1
+        kind = kept(jnp.where(ok_y, field_w[0, x], 0.0), side, 0)
+        solid_w[x, 8:32] = jnp.where(kind == 2.0, 1.0, 0.0)
+        fluid = kind == 1.0
         scale_w[x] = jnp.where(fluid, 1.0, 0.0)
-        press_a[x, 8:32] = jnp.where(fluid, old_w[x], 0.0)
+        press_a[x, 8:32] = jnp.where(fluid, field_w[1, x], 0.0)
     for x in range(1, WIDE_X - 1):
         middle = solid_w[x, 8:32]
         closed = (
@@ -403,40 +465,37 @@
 
     sub8 = iota((8, 128), 0)
 
-    def kept(v, dx, dy):
-        if dx:
-            v = jnp.where(inside_x[dx], v, 0.0)
-        if dy:
-            v = jnp.where(inside_y[dy], v, 0.0)
-        return v
-
     def at_first(v, row):
         return jnp.where(sub8 == 0, v + row, v)
 
     speed_f = speed_w.reshape(3 * 10 * 24, 128)
-    flag_f = flag_w.reshape(WIDE_X * 24, 128)
-
-    def normalised(sums4, kind, dx, dy):
+    field_f = flat_rows(field_w)
+
+    def normalised(sums4, kind, dx, dy, components=(0, 1, 2)):
         inverse = 1.0 / jnp.maximum(sums4[0], MASS_FLOOR)
         result = []
-        for k in range(3):
+        for k in components:
             u = sums4[k + 1] * inverse
             if k == 2:
                 u = u - TIME_STEP * GRAVITY
-            result.append(kept(jnp.where(kind == 2, 0.0, u), dx, dy))
+            result.append(kept(jnp.where(kind == 2.0, 0.0, u), dx, dy))
         return result
 
-    minus_rows, zero_rows, plus_rows, below_columns, upper_columns = [], [], [], [], []
+    minus_rows, below_columns = [None] * 4, [None] * 4
+    for i, k in enumerate((0, 1)):
+        minus_rows[k] = at_first(
+            kept(arrive0[4 + i], -1, 0), kept(arrive4[1, k : k + 1], -1, -1)
+        )
+    for i, k in enumerate((0, 2)):
+        below_columns[k] = at_first(
+            kept(arrive2[4 + i], 0, -1), kept(arrive4[1, 4 + k : 5 + k], -1, -1)
+        )
+    plus_rows, upper_columns = [], []
     for k in range(4):
-        minus_rows.append(
-            at_first(
-                kept(arrive0[2 * k], -1, 0), kept(arrive4[1, k : k + 1], -1, -1)
-            )
-        )
-        first = nodes[pl.ds(k * 72, 8), :] + kept(arrive0[2 * k + 1], -1, 0)
+        first = nodes[pl.ds(k * 72, 8), :] + kept(arrive0[k], -1, 0)
         nodes[pl.ds(k * 72, 8), :] = first
         column = at_first(
-            kept(arrive2[2 * k + 1], 0, -1), kept(arrive4[0, k : k + 1], -1, -1)
+            kept(arrive2[k], 0, -1), kept(arrive4[0, k : k + 1], -1, -1)
         )
         nodes[pl.ds(k * 72, 8, stride=8), :] = (
             nodes[pl.ds(k * 72, 8, stride=8), :] + column
@@ -444,19 +503,14 @@
         plus_rows.append(
             at_first(
                 nodes[pl.ds((k * 9 + 8) * 8, 8), :] + kept(arrive1[k], 1, 0),
-                kept(arrive2[8, k : k + 1], 0, -1)
+                kept(arrive2[6, k : k + 1], 0, -1)
                 + kept(arrive6[0, 4 + k : 5 + k], 1, -1),
-            )
-        )
-        below_columns.append(
-            at_first(
-                kept(arrive2[2 * k], 0, -1), kept(arrive4[1, 4 + k : 5 + k], -1, -1)
             )
         )
         upper_columns.append(
             at_first(
                 column8[k] + kept(arrive3[k], 0, 1),
-                kept(arrive0[8, k : k + 1], -1, 0) + kept(arrive5[0, k : k + 1], -1, 1),
+                kept(arrive0[6, k : k + 1], -1, 0) + kept(arrive5[0, k : k + 1], -1, 1),
             )
         )
     corner = (
@@ -474,43 +528,37 @@
         else:
             sums4 = [nodes[pl.ds((k * 9 + x) * 8, 8), :] for k in range(4)]
             side = 0
-        u = normalised(sums4, flag_w[x + 5, 8:16], side, 0)
-        for k in range(3):
+        wanted = (0,) if x == -1 else (0, 1, 2)
+        u = normalised(sums4, field_w[0, x + 5, 8:16], side, 0, wanted)
+        for k in wanted:
             speed_w[k, x + 1, 8:16] = u[k]
-    for columns, y, side in ((below_columns, 7, -1), (upper_columns, 16, 1)):
-        u = normalised(columns, flag_f[pl.ds(5 * 24 + y, 8, stride=24), :], 0, side)
-        for k in range(3):
-            speed_f[pl.ds((k * 10 + 1) * 24 + y, 8, stride=24), :] = u[k]
-    u = normalised(
-        [corner[k : k + 1] for k in range(4)], flag_w[13, 16:17], 1, 1
-    )
+    for columns, y, side, wanted in (
+        (below_columns, 7, -1, (1,)),
+        (upper_columns, 16, 1, (0, 1, 2)),
+    ):
+        kind = field_f[pl.ds(5 * 24 + y, 8, stride=24), :]
+        u = normalised(columns, kind, 0, side, wanted)
+        for i, k in enumerate(wanted):
+            speed_f[pl.ds((k * 10 + 1) * 24 + y, 8, stride=24), :] = u[i]
+    u = normalised([corner[k : k + 1] for k in range(4)], field_w[0, 13, 16:17], 1, 1)
     for k in range(3):
         speed_w[k, 9, 16:17] = u[k]
 
     for x in range(8):
-        source_w[x + 5, 8:16] = 0.5 * (
+        source_w[0, x + 5, 8:16] = 0.5 * (
             speed_w[0, x + 2, 8:16]
             - speed_w[0, x, 8:16]
             + (speed_w[1, x + 1, 9:17] - speed_w[1, x + 1, 7:15])
             + (above_z(speed_w[2, x + 1, 8:16]) - below_z(speed_w[2, x + 1, 8:16]))
         )
 
-    margins = []
-    for number in range(8):
-        (s0, s1), (t0, t1), tile = SOURCE_PARTS[number]
-        margins.append(
-            copy_to(
-                number,
-                3,
-                source_w.at[pl.ds(s0, s1 - s0), pl.ds(8, 8)],
-                source_w.at[pl.ds(t0, t1 - t0), pl.ds(8 * tile, 8)],
-            )
-        )
+    margins = halo(2, source_w, source_out, source_in, SOURCE_REACH)
     for copy in margins:
         copy.start()
     lax.fori_loop(8, 16, slot_rows, 0)
     for copy in margins:
         copy.wait_recv()
+    unpack(source_w, source_in, SOURCE_REACH)
 
     old, new = press_a, press_b
     for sweep in range(ITERS):
@@ -526,7 +574,7 @@
                 + above_z(middle)
             )
             scale = scale_w[x]
-            new[x, 8:32] = jnp.where(scale > 0.0, scale * (near - source_w[x]), 0.0)
+            new[x, 8:32] = jnp.where(scale > 0.0, scale * (near - source_w[0, x]), 0.0)
         old, new = new, old
     for x in range(8):
         press_o[x] = old[x + 5, 16:24]
@@ -548,26 +596,58 @@
             settled[k, x] = speed_w[k, x + 1, 8:24] - jnp.where(fluid, 0.5 * slopes[k], 0.0)
 
     odd8 = (iota((8, 128), 0) & 1) == 1
-    for xb in range(2):
-        rows = pl.ds(32 * xb, 32)
+    sub8 = iota((8, 128), 0)
+    lane8 = iota((8, 128), 1)
+
+    def table_row(k, ix, iy, j):
+        return pl.ds(8 * (((k * 5 + ix) * 5 + iy) * 2 + j), 8)
+
+    def sample_blocks(xb, carry):
+        for k in range(3):
+            for ix in range(5):
+                for iy in range(5):
+                    even = jnp.broadcast_to(settled[k, 4 * xb + ix, iy : iy + 1], (8, 128))
+                    odd = jnp.broadcast_to(settled[k, 4 * xb + ix, iy + 4 : iy + 5], (8, 128))
+                    table = jnp.where(odd8, odd, even)
+                    tables[table_row(k, ix, iy, 0), :] = table
+                    tables[table_row(k, ix, iy, 1), :] = above_z(table) - table
+        return lax.fori_loop(0, 4, functools.partial(sample_rows, xb), carry)
+
+    def sample_rows(xb, g, carry):
+        start = pl.multiple_of(32 * xb + 8 * g, 8)
+        rows = pl.ds(start, 8)
         cell = cell_v[rows, :]
         alive = alive_v[rows, :]
         qx, qy = cell >> 4, (cell >> 2) & 3
-        z = ((sub32 >> 1) << 3) + ((lane32 >> 6) << 2) + (cell & 3)
+        z = ((4 * g + (sub8 >> 1)) << 3) + ((lane8 >> 6) << 2) + (cell & 3)
+        at_x = [qx == i for i in range(4)]
+        at_y = [qy == i for i in range(4)]
         f = [off_v[d, rows, :] for d in range(3)]
-        speeds, offsets = [], []
+
+        def record_row(number):
+            return pl.ds(pl.multiple_of(number * 64 + start, 8), 8)
+
+        moving = dest_v[rows, :]
+
+        def one_of(*numbers):
+            hit = moving == numbers[0]
+            for number in numbers[1:]:
+                hit = hit | (moving == number)
+            return jnp.where(hit, 8, 0)
+
+        place = (
+            4 * xb + qx - one_of(1, 5, 6) + one_of(2, 7, 8),
+            ((sub8 & 1) << 2) + qy - one_of(3, 5, 7) + one_of(4, 6, 8),
+            z,
+        )
         for k in range(3):
             pick_x = [[None] * 4, [None] * 4]
             for ix in range(5):
                 pick_y = [[None] * 2, [None] * 2]
                 for iy in range(5):
-                    even = jnp.broadcast_to(settled[k, 4 * xb + ix, iy : iy + 1], (8, 128))
-                    odd = jnp.broadcast_to(settled[k, 4 * xb + ix, iy + 4 : iy + 5], (8, 128))
-                    table = jnp.where(odd8, odd, even)
-                    rise = above_z(table) - table
                     got = [
-                        jnp.take_along_axis(jnp.concatenate([t] * 4, axis=0), z, axis=1)
-                        for t in (table, rise)
+                        jnp.take_along_axis(tables[table_row(k, ix, iy, j), :], z, axis=1)
+                        for j in range(2)
                     ]
                     for o in range(2):
                         if not 0 <= iy - o < 4:
@@ -577,7 +657,7 @@
                             pick_y[o][j] = (
                                 got[j]
                                 if held is None
-                                else jnp.where(qy == iy - o, got[j], held)
+                                else jnp.where(at_y[iy - o], got[j], held)
                             )
                 flat = pick_y[0] + pick_y[1]
                 for o in range(2):
@@ -586,21 +666,19 @@
                     for j in range(4):
                         held = pick_x[o][j]
                         pick_x[o][j] = (
-                            flat[j] if held is None else jnp.where(qx == ix - o, flat[j], held)
+                            flat[j] if held is None else jnp.where(at_x[ix - o], flat[j], held)
                         )
             value, along_y, along_z = [], [], []
             for o in range(2):
-                a0, d0, a1, d1_ = pick_x[o]
-                v0 = a0 + f[2] * d0
-                v1 = a1 + f[2] * d1_
+                a0, rise0, a1, rise1 = pick_x[o]
+                v0 = a0 + f[2] * rise0
+                v1 = a1 + f[2] * rise1
                 along_y.append(v1 - v0)
                 value.append(v0 + f[1] * (v1 - v0))
-                along_z.append(d0 + f[1] * (d1_ - d0))
+                along_z.append(rise0 + f[1] * (rise1 - rise0))
             along_x = value[1] - value[0]
             speed = (value[0] + f[0] * along_x) * alive
             offset = f[k] + TIME_STEP * speed
-            speeds.append(speed)
-            offsets.append(offset)
             slope = (
                 along_x * alive,
                 (along_y[0] + f[0] * (along_y[1] - along_y[0])) * alive,
@@ -608,55 +686,37 @@
             )
             off_o[k, rows, :] = offset
             vel_o[k, rows, :] = speed
-            records[pl.ds((3 + k) * 64 + 32 * xb, 32), :] = speed
+            records[record_row(k), :] = place[k].astype(F32) + offset
+            records[record_row(3 + k), :] = speed
             for b in range(3):
                 aff_o[3 * k + b, rows, :] = slope[b]
-                records[pl.ds((6 + 3 * k + b) * 64 + 32 * xb, 32), :] = slope[b]
-        moving = dest_v[rows, :]
-
-        def one_of(*numbers):
-            hit = moving == numbers[0]
-            for number in numbers[1:]:
-                hit = hit | (moving == number)
-            return jnp.where(hit, 8, 0)
-
-        place = (
-            4 * xb + qx - one_of(1, 5, 6) + one_of(2, 7, 8),
-            None,
-            z,
-        )
-        row_y = (sub32 & 1) << 2
-        place = (
-            place[0],
-            row_y + qy - one_of(3, 5, 7) + one_of(4, 6, 8),
-            z,
-        )
-        for d in range(3):
-            records[pl.ds(d * 64 + 32 * xb, 32), :] = place[d].astype(F32) + offsets[d]
-        records[pl.ds(15 * 64 + 32 * xb, 32), :] = jnp.zeros((32, 128), F32)
+                records[record_row(6 + 3 * k + b), :] = slope[b]
+        records[record_row(15), :] = jnp.zeros((8, 128), F32)
+        return carry
+
+    lax.fori_loop(0, 2, sample_blocks, 0)
 
     def parcel_rows(step, carry):
         for j in range(4):
             r = 4 * step + j
             record = records[pl.ds(r, 16, stride=64), :]
             high, low = two_parts(record)
-            moving = jnp.broadcast_to(dest_v[pl.ds(r, 1), :], (16, 128))
+            moving = jnp.broadcast_to(dest_v[pl.ds(r, 1), :].astype(F32), (16, 128)).astype(BF16)
             lanes = pl.ds(pl.multiple_of(r * 128, 128), 128)
             for number in range(8):
-                picked = (moving == number + 1).astype(F32).astype(BF16)
-                parcels[pl.ds(32 * number, 16), lanes] = high * picked
-                parcels[pl.ds(32 * number + 16, 16), lanes] = low * picked
+                hit = moving == number + 1
+                parcels[pl.ds(32 * number, 16), lanes] = jnp.where(hit, high, 0.0).astype(BF16)
+                parcels[pl.ds(32 * number + 16, 16), lanes] = jnp.where(hit, low, 0.0).astype(BF16)
         return carry
 
     lax.fori_loop(0, 16, parcel_rows, 0)
+    placed = dot_last(parcels[...], slot_onehot[...])
     leaving = [None] * 8
-    for half in (1, 0):
-        placed = dot_last(parcels[pl.ds(128 * half, 128), :], slot_onehot[...])
-        for j in range(4):
-            number = 4 * half + j
-            outgoing[number] = placed[32 * j : 32 * j + 16] + placed[32 * j + 16 : 32 * j + 32]
-            leaving[number] = copy_to(number, 4, outgoing.at[number], incoming.at[number])
-            leaving[number].start()
+    for number in (4, 5, 6, 7, 0, 1, 2, 3):
+        first = 32 * number
+        outgoing[number] = placed[first : first + 16] + placed[first + 16 : first + 32]
+        leaving[number] = copy_to(number, 3, outgoing.at[number], incoming.at[number])
+        leaving[number].start()
 
     for copy in exchanges + sums + margins:
         copy.wait_send()
@@ -670,6 +730,16 @@
             rec_f[pl.ds(2 * number + half, 15, stride=16), :] = arrived[
                 0:15, 128 * half : 128 * half + 128
             ]
+
+
+def write_out(*refs):
+    copies = [
+        pltpu.make_async_copy(refs[i], refs[5 + i], refs[10].at[i]) for i in range(5)
+    ]
+    for copy in copies:
+        copy.start()
+    for copy in copies:
+        copy.wait()
 
 
 def in_rows(a):
@@ -709,15 +779,14 @@
     def f32(*shape):
         return pltpu.VMEM(shape, F32)
 
+    def halos(count, reach):
+        rows = [8 * reach, 8 * (reach + 1)] + [8 * corner_tiles(n, reach) for n in range(4, 8)]
+        return [f32(count, n, 128) for n in rows]
+
+    shapes = ((3, 64, 128), (3, 64, 128), (9, 64, 128), (8, 8, 128), (15, 16, 128))
     outs = pl.pallas_call(
         functools.partial(kernel, nx, ny),
-        out_shape=[
-            jax.ShapeDtypeStruct((3, 64, 128), F32),
-            jax.ShapeDtypeStruct((3, 64, 128), F32),
-            jax.ShapeDtypeStruct((9, 64, 128), F32),
-            jax.ShapeDtypeStruct((8, 8, 128), F32),
-            jax.ShapeDtypeStruct((15, 16, 128), F32),
-        ],
+        out_shape=[pltpu.VMEM(shape, F32) for shape in shapes],
         in_specs=[anywhere] * 9,
         out_specs=[vmem] * 5,
         scratch_shapes=[
@@ -728,8 +797,8 @@
             pltpu.VMEM((2, 2, 32), I32),
             pltpu.VMEM((64, 128), I32),
             pltpu.VMEM((64, 128), I32),
-            pltpu.VMEM((WIDE_X, 24, 128), I32),
-            f32(WIDE_X, 24, 128),
+            pltpu.VMEM((8, 8, 128), I32),
+            f32(2, WIDE_X, 24, 128),
             f32(64, 128),
             pltpu.VMEM((64, 128), I32),
             f32(32 * 64, 128),
@@ -737,46 +806,65 @@
             f32(10 * 10 * 16, 128),
             f32(4 * 9 * 8, 128),
             f32(4, 8, 128),
-            f32(9, 8, 128),
+            f32(7, 8, 128),
             f32(5, 8, 128),
-            f32(9, 8, 128),
+            f32(7, 8, 128),
             f32(5, 8, 128),
             f32(2, 8, 128),
             f32(1, 8, 128),
         ]
         + [f32(tiles, 8, 128) for tiles in SUM_TILES]
         + [
+            halos(2, FIELD_REACH),
+            halos(2, FIELD_REACH),
+            halos(1, SOURCE_REACH),
+            halos(1, SOURCE_REACH),
             f32(3, 10, 24, 128),
-            f32(WIDE_X, 24, 128),
+            f32(1, WIDE_X, 24, 128),
             f32(WIDE_X, 24, 128),
             f32(WIDE_X, 40, 128),
             f32(WIDE_X, 40, 128),
             f32(WIDE_X, 40, 128),
             f32(3, 9, 16, 128),
+            f32(150 * 8, 128),
             pltpu.VMEM((256, 8192), BF16),
             pltpu.VMEM((256, 8192), BF16),
             f32(16 * 64, 128),
             f32(8, 16, 256),
             f32(8, 16, 256),
             pltpu.SemaphoreType.DMA((9,)),
-            pltpu.SemaphoreType.DMA((40,)),
-            pltpu.SemaphoreType.DMA((40,)),
+            pltpu.SemaphoreType.DMA((32,)),
+            pltpu.SemaphoreType.DMA((32,)),
         ],
         compiler_params=pltpu.CompilerParams(
-            collective_id=0, has_side_effects=True, vmem_limit_bytes=48 * 1024 * 1024
+            collective_id=0, has_side_effects=True, vmem_limit_bytes=60 * 1024 * 1024
         ),
         name="substep",
     )(
-        in_rows(cell_offset),
-        in_rows(velocity),
-        in_rows(affine),
-        in_rows(cell_index),
-        counts,
-        cell_flags,
-        old_pressure,
-        in_rows(destination),
-        in_rows(dest_slot),
+        *[
+            pltpu.with_memory_space_constraint(a, pltpu.HBM)
+            for a in (
+                in_rows(cell_offset),
+                in_rows(velocity),
+                in_rows(affine),
+                in_rows(cell_index),
+                counts,
+                cell_flags,
+                old_pressure,
+                in_rows(destination),
+                in_rows(dest_slot),
+            )
+        ]
     )
+    outs = pl.pallas_call(
+        write_out,
+        out_shape=[jax.ShapeDtypeStruct(shape, F32) for shape in shapes],
+        in_specs=[vmem] * 5,
+        out_specs=[anywhere] * 5,
+        scratch_shapes=[pltpu.SemaphoreType.DMA((5,))],
+        compiler_params=pltpu.CompilerParams(vmem_limit_bytes=60 * 1024 * 1024),
+        name="write_out",
+    )(*[pltpu.with_memory_space_constraint(a, pltpu.VMEM) for a in outs])
     return (
         from_rows(outs[0]),
         from_rows(outs[1]),

time: 63.2 us -> 40.7 us (0.64)
  Pallas kernels: 51.5 us -> 39.9 us
  local copies, waits for them, and re-layouts: 10.5 us -> 0 us
    pallas_call x1 -> x2, Pallas kernels: 51.5 us -> 39.9 us  [the longest x1 39 us: on_device(): pl.pallas_call(functools.partial(kernel, nx, ny), out_shape=[pltpu.VMEM(s...]
    unnamed x23 -> x0, local copies, waits for them, and re-layouts: 10.5 us -> none
where the time goes in v1:
time: 40.7 us; the launch traced here: 40.5 us
  Pallas kernels  39.9 us (98%)
  between operations  0.64 us (2%)
    pallas_call x1, Pallas kernels, on_device(): pl.pallas_call(functools.partial(kernel, nx, ny), out_shape=[pltpu.VMEM(s...  39 us
    pallas_call x1, Pallas kernels, on_device(): pl.pallas_call(write_out, out_shape=[jax.ShapeDtypeStruct(shape, F32) for...  0.87 us

profile of v1, /device:TPU:1, one launch (start us, length us, event | category | flops | bytes accessed | tf_op | source)
XLA Modules:
  0.0 40.5 jit_solution(1262571539175430371)
XLA Ops:
  0.6 39.0 %substep.1 = (f32[3,64,128]{2,1,0:T(8,128)S(1)}, f32[3,64,128]{2,1,0:T(8,128)S(1)}, f32[9,64,128]{2,1,0:T(8,128)S(1)}, f32[8,8,128]{2,1,0:T(8,128)S(1)}, f32[15,16,128]{2,1,0:T(8,128)S(1)}) custom-call(f32[3,64,128]{2,1,0:T(8,128)} %bitcast.47, f32[3,64,128]{2,1,0:T(8,128)} %bitcast.48, f32[9,64,128]{2,1,0:T(8,128)} %bitcast.46, s32[64,128]{1,0:T(8,128)} %bitcast.49, ...), custom_call_target="tpu_custom_call" | custom-call | tf_op jit(solution)/shard_map/substep/pallas_call | solution.py:787
  39.7 0.9 %write_out.1 = (f32[3,64,128]{2,1,0:T(8,128)}, f32[3,64,128]{2,1,0:T(8,128)}, f32[9,64,128]{2,1,0:T(8,128)}, f32[8,8,128]{2,1,0:T(8,128)}, f32[15,16,128]{2,1,0:T(8,128)}) custom-call(f32[3,64,128]{2,1,0:T(8,128)S(1)} %get-tuple-element.15.refs_0_, f32[3,64,128]{2,1,0:T(8,128)S(1)} %get-tuple-element.16.refs_1_, ...), custom_call_target="tpu_custom_call" | custom-call | tf_op jit(solution)/shard_map/write_out/pallas_call | solution.py:859

commit v2 on v1

--- a/solution.py
+++ b/solution.py
@@ -62,7 +62,8 @@
 def matches(row, count):
     places = iota((count, 128), 0).astype(F32).astype(BF16)
     wanted = jnp.broadcast_to(row.astype(F32), (count, 128)).astype(BF16)
-    return jnp.where(places == wanted, 1.0, 0.0).astype(BF16)
+    one, zero = jnp.ones((count, 128), BF16), jnp.zeros((count, 128), BF16)
+    return jnp.where(places == wanted, one, zero)
 
 
 def dot_last(a, b):
@@ -85,6 +86,20 @@
 
 def cell_row(x, y, ox, oy, k):
     return ((x + 1) * 10 + (y + 1)) * 16 + 8 * ox + 4 * oy + k
+
+
+class Neighbourly:
+    def __init__(self, copy, goes, comes):
+        self.copy, self.goes, self.comes = copy, goes, comes
+
+    def start(self):
+        pl.when(self.goes)(self.copy.start)
+
+    def wait_send(self):
+        pl.when(self.goes)(self.copy.wait_send)
+
+    def wait_recv(self):
+        pl.when(self.comes)(self.copy.wait_recv)
 
 
 def kernel(
@@ -163,7 +178,7 @@
 
     def copy_to(number, stage, src, dst):
         dx, dy = STEPS[number]
-        return pltpu.make_async_remote_copy(
+        copy = pltpu.make_async_remote_copy(
             src_ref=src,
             dst_ref=dst,
             send_sem=send_sem.at[8 * stage + number],
@@ -171,6 +186,9 @@
             device_id=(where_x[dx], where_y[dy]),
             device_id_type=MESH,
         )
+        goes = inside_x[dx] & inside_y[dy]
+        comes = inside_x[-dx] & inside_y[-dy]
+        return Neighbourly(copy, goes, comes)
 
     def flat_rows(field):
         return field.reshape(field.shape[0] * WIDE_X * 24, 128)
@@ -253,9 +271,17 @@
 
     barrier = pltpu.get_barrier_semaphore()
     for dx, dy in STEPS:
-        pl.semaphore_signal(
-            barrier, inc=1, device_id=(where_x[dx], where_y[dy]), device_id_type=MESH
-        )
+        pl.when(inside_x[dx] & inside_y[dy])(
+            functools.partial(
+                pl.semaphore_signal,
+                barrier,
+                inc=1,
+                device_id=(where_x[dx], where_y[dy]),
+                device_id_type=MESH,
+            )
+        )
+    near_x = 1 + inside_x[1].astype(I32) + inside_x[-1].astype(I32)
+    near_y = 1 + inside_y[1].astype(I32) + inside_y[-1].astype(I32)
 
     zero_tile = jnp.zeros((8, 128), F32)
     for x in range(WIDE_X):
@@ -268,7 +294,7 @@
     for half in (0, 8):
         cells[pl.ds(cell_row(-1, 7, 0, 0, 0) + half, 8), :] = zero_tile
 
-    pl.semaphore_wait(barrier, 8)
+    pl.semaphore_wait(barrier, near_x * near_y - 1)
     loads[0].wait()
     loads[1].wait()
 
@@ -701,12 +727,12 @@
             r = 4 * step + j
             record = records[pl.ds(r, 16, stride=64), :]
             high, low = two_parts(record)
-            moving = jnp.broadcast_to(dest_v[pl.ds(r, 1), :].astype(F32), (16, 128)).astype(BF16)
+            both = jnp.concatenate([high, low], axis=0)
+            moving = jnp.broadcast_to(dest_v[pl.ds(r, 1), :].astype(F32), (32, 128)).astype(BF16)
             lanes = pl.ds(pl.multiple_of(r * 128, 128), 128)
             for number in range(8):
-                hit = moving == number + 1
-                parcels[pl.ds(32 * number, 16), lanes] = jnp.where(hit, high, 0.0).astype(BF16)
-                parcels[pl.ds(32 * number + 16, 16), lanes] = jnp.where(hit, low, 0.0).astype(BF16)
+                hit = moving == jnp.full((32, 128), number + 1, BF16)
+                parcels[pl.ds(32 * number, 32), lanes] = jnp.where(hit, both, jnp.zeros_like(both))
         return carry
 
     lax.fori_loop(0, 16, parcel_rows, 0)
@@ -723,7 +749,8 @@
 
     rec_f = rec_o.reshape(15 * 16, 128)
     for number in (4, 5, 6, 7, 0, 1, 2, 3):
-        leaving[number].wait()
+        leaving[number].wait_recv()
+        leaving[number].wait_send()
         dx, dy = STEPS[number]
         arrived = kept(incoming[number], -dx, -dy)
         for half in range(2):

time: 40.7 us -> 30.7 us (0.75)
  Pallas kernels: 39.9 us -> 29.8 us
    pallas_call x1, Pallas kernels: 39 us -> 29 us  [on_device(): pl.pallas_call(functools.partial(kernel, nx, ny), out_shape=[pltpu.VMEM(s...]
where the time goes in v2:
time: 30.7 us; the launch traced here: 30.5 us
  Pallas kernels  29.8 us (97%)
  between operations  0.64 us (2%)
    pallas_call x1, Pallas kernels, on_device(): pl.pallas_call(functools.partial(kernel, nx, ny), out_shape=[pltpu.VMEM(s...  29 us
    pallas_call x1, Pallas kernels, on_device(): pl.pallas_call(write_out, out_shape=[jax.ShapeDtypeStruct(shape, F32) for...  0.87 us

profile of v2, /device:TPU:1, one launch (start us, length us, event | category | flops | bytes accessed | tf_op | source)
XLA Modules:
  0.0 30.5 jit_solution(16426167621464104704)
XLA Ops:
  0.6 29.0 %substep.1 = (f32[3,64,128]{2,1,0:T(8,128)S(1)}, f32[3,64,128]{2,1,0:T(8,128)S(1)}, f32[9,64,128]{2,1,0:T(8,128)S(1)}, f32[8,8,128]{2,1,0:T(8,128)S(1)}, f32[15,16,128]{2,1,0:T(8,128)S(1)}) custom-call(f32[3,64,128]{2,1,0:T(8,128)} %bitcast.47, f32[3,64,128]{2,1,0:T(8,128)} %bitcast.48, f32[9,64,128]{2,1,0:T(8,128)} %bitcast.46, s32[64,128]{1,0:T(8,128)} %bitcast.49, ...), custom_call_target="tpu_custom_call" | custom-call | tf_op jit(solution)/shard_map/substep/pallas_call | solution.py:814
  29.6 0.9 %write_out.1 = (f32[3,64,128]{2,1,0:T(8,128)}, f32[3,64,128]{2,1,0:T(8,128)}, f32[9,64,128]{2,1,0:T(8,128)}, f32[8,8,128]{2,1,0:T(8,128)}, f32[15,16,128]{2,1,0:T(8,128)}) custom-call(f32[3,64,128]{2,1,0:T(8,128)S(1)} %get-tuple-element.15.refs_0_, f32[3,64,128]{2,1,0:T(8,128)S(1)} %get-tuple-element.16.refs_1_, ...), custom_call_target="tpu_custom_call" | custom-call | tf_op jit(solution)/shard_map/write_out/pallas_call | solution.py:886

commit v3 on v2

--- a/solution.py
+++ b/solution.py
@@ -72,15 +72,15 @@
 
 def blocks_exchanged(parts):
     parts = list(parts)
-    group = iota(parts[0].shape, 1) >> 3
-    for bit in (1, 2, 4, 8):
+    group = iota(parts[0].shape, 1) >> 4
+    for bit in (1, 2, 4):
         upper = (group & bit) != 0
-        for i in range(16):
+        for i in range(8):
             if i & bit:
                 continue
             low, high = parts[i], parts[i | bit]
-            parts[i] = jnp.where(upper, pltpu.roll(high, 8 * bit, 1), low)
-            parts[i | bit] = jnp.where(upper, high, pltpu.roll(low, 128 - 8 * bit, 1))
+            parts[i] = jnp.where(upper, pltpu.roll(high, 16 * bit, 1), low)
+            parts[i | bit] = jnp.where(upper, high, pltpu.roll(low, 128 - 16 * bit, 1))
     return parts
 
 
@@ -327,7 +327,10 @@
         )
         number_in_block = cell_v[pl.ds(r0, 32), :]
         bin_v[pl.ds(r0, 32), :] = (
-            ((number_in_block >> 2) << 3) + ((lane32 >> 6) << 2) + (number_in_block & 3)
+            ((number_in_block >> 2) << 4)
+            + (((sub32 >> 1) & 1) << 3)
+            + ((lane32 >> 6) << 2)
+            + (number_in_block & 3)
         )
 
     def deposit(step, carry):
@@ -362,31 +365,37 @@
 
     def bin_column(col, carry):
         xb, yb = col // 2, lax.rem(col, 2)
-        for zt in range(16):
-            r = 32 * xb + yb + 2 * zt
-            values = quant[pl.ds(r, 32, stride=64), :]
-            high, low = two_parts(values)
-            onehot = matches(bin_v[pl.ds(r, 1), :], 128)
-            total = dot_last(jnp.concatenate([high, low], axis=0), onehot)
-            binned[zt] = total[0:32] + total[32:64]
-        first_z = (iota((8, 128), 1) & 7) == 0
-        for g in range(2):
-            parts = []
-            for zt in range(16):
-                same = pltpu.roll(binned[zt, 16 + 8 * g : 24 + 8 * g], 1, 1)
-                before = (
-                    pltpu.roll(binned[zt - 1, 16 + 8 * g : 24 + 8 * g], 121, 1) if zt else 0.0
+        first_z = (iota((16, 128), 1) & 15) == 0
+        before = [0.0, 0.0]
+        for pair in range(8):
+            sides, hots = [], []
+            for j in range(2):
+                r = 32 * xb + yb + 4 * pair + 2 * j
+                high, low = two_parts(quant[pl.ds(r, 32, stride=64), :])
+                sides.append(jnp.concatenate([high, low], axis=0))
+                hots.append(matches(bin_v[pl.ds(r, 1), :], 256))
+            total = dot_last(jnp.concatenate(sides, axis=1), jnp.concatenate(hots, axis=1))
+            total = total[0:32] + total[32:64]
+            for h in range(2):
+                lower = total[0:16, 128 * h : 128 * h + 128]
+                upper = total[16:32, 128 * h : 128 * h + 128]
+                carried = before[h]
+                before[h] = pltpu.roll(upper, 113, 1)
+                binned[2 * pair + h] = lower + jnp.where(
+                    first_z, carried, pltpu.roll(upper, 1, 1)
                 )
-                parts.append(
-                    binned[zt, 8 * g : 8 * g + 8] + jnp.where(first_z, before, same)
+        for h in range(2):
+            for g in range(2):
+                parts = blocks_exchanged(
+                    [binned[2 * pair + h, 8 * g : 8 * g + 8] for pair in range(8)]
                 )
-            parts = blocks_exchanged(parts)
-            for q in range(16):
-                start = ((4 * xb + q // 4 + 1) * 10 + 4 * yb + q % 4 + 1) * 16 + 8 * g
-                cells[pl.ds(pl.multiple_of(start, 8), 8), :] = parts[q]
+                for i in range(8):
+                    q = 8 * h + i
+                    start = ((4 * xb + q // 4 + 1) * 10 + 4 * yb + q % 4 + 1) * 16 + 8 * g
+                    cells[pl.ds(pl.multiple_of(start, 8), 8), :] = parts[i]
         return carry
 
-    lax.fori_loop(0, 4, bin_column, 0)
+    lax.fori_loop(0, 4, bin_column, 0, unroll=4)
 
     for k in range(4):
         for x in range(9):
@@ -637,7 +646,7 @@
                     table = jnp.where(odd8, odd, even)
                     tables[table_row(k, ix, iy, 0), :] = table
                     tables[table_row(k, ix, iy, 1), :] = above_z(table) - table
-        return lax.fori_loop(0, 4, functools.partial(sample_rows, xb), carry)
+        return lax.fori_loop(0, 4, functools.partial(sample_rows, xb), carry, unroll=4)
 
     def sample_rows(xb, g, carry):
         start = pl.multiple_of(32 * xb + 8 * g, 8)
@@ -718,13 +727,8 @@
                 aff_o[3 * k + b, rows, :] = slope[b]
                 records[record_row(6 + 3 * k + b), :] = slope[b]
         records[record_row(15), :] = jnp.zeros((8, 128), F32)
-        return carry
-
-    lax.fori_loop(0, 2, sample_blocks, 0)
-
-    def parcel_rows(step, carry):
-        for j in range(4):
-            r = 4 * step + j
+        for j in range(8):
+            r = start + j
             record = records[pl.ds(r, 16, stride=64), :]
             high, low = two_parts(record)
             both = jnp.concatenate([high, low], axis=0)
@@ -735,7 +739,9 @@
                 parcels[pl.ds(32 * number, 32), lanes] = jnp.where(hit, both, jnp.zeros_like(both))
         return carry
 
-    lax.fori_loop(0, 16, parcel_rows, 0)
+    lax.fori_loop(0, 2, sample_blocks, 0)
+
+
     placed = dot_last(parcels[...], slot_onehot[...])
     leaving = [None] * 8
     for number in (4, 5, 6, 7, 0, 1, 2, 3):
@@ -829,7 +835,7 @@
             f32(64, 128),
             pltpu.VMEM((64, 128), I32),
             f32(32 * 64, 128),
-            f32(16, 32, 128),
+            f32(16, 16, 128),
             f32(10 * 10 * 16, 128),
             f32(4 * 9 * 8, 128),
             f32(4, 8, 128),

time: 30.7 us -> 30.8 us (level)
  the two profiles are of different devices: /device:TPU:1 before, /device:TPU:231 now
where the time goes in v3:
time: 30.8 us; the launch traced here: 30.6 us
  Pallas kernels  30 us (97%)
  between operations  0.64 us (2%)
    pallas_call x1, Pallas kernels, on_device(): pl.pallas_call(functools.partial(kernel, nx, ny), out_shape=[pltpu.VMEM(s...  29.1 us
    pallas_call x1, Pallas kernels, on_device(): pl.pallas_call(write_out, out_shape=[jax.ShapeDtypeStruct(shape, F32) for...  0.87 us

profile of v3, /device:TPU:231, one launch (start us, length us, event | category | flops | bytes accessed | tf_op | source)
XLA Modules:
  0.0 30.6 jit_solution(12408516739849980144)
XLA Ops:
  0.6 29.1 %substep.1 = (f32[3,64,128]{2,1,0:T(8,128)S(1)}, f32[3,64,128]{2,1,0:T(8,128)S(1)}, f32[9,64,128]{2,1,0:T(8,128)S(1)}, f32[8,8,128]{2,1,0:T(8,128)S(1)}, f32[15,16,128]{2,1,0:T(8,128)S(1)}) custom-call(f32[3,64,128]{2,1,0:T(8,128)} %bitcast.47, f32[3,64,128]{2,1,0:T(8,128)} %bitcast.48, f32[9,64,128]{2,1,0:T(8,128)} %bitcast.46, s32[64,128]{1,0:T(8,128)} %bitcast.49, ...), custom_call_target="tpu_custom_call" | custom-call | tf_op jit(solution)/shard_map/substep/pallas_call | solution.py:820
  29.7 0.9 %write_out.1 = (f32[3,64,128]{2,1,0:T(8,128)}, f32[3,64,128]{2,1,0:T(8,128)}, f32[9,64,128]{2,1,0:T(8,128)}, f32[8,8,128]{2,1,0:T(8,128)}, f32[15,16,128]{2,1,0:T(8,128)}) custom-call(f32[3,64,128]{2,1,0:T(8,128)S(1)} %get-tuple-element.15.refs_0_, f32[3,64,128]{2,1,0:T(8,128)S(1)} %get-tuple-element.16.refs_1_, ...), custom_call_target="tpu_custom_call" | custom-call | tf_op jit(solution)/shard_map/write_out/pallas_call | solution.py:892

commit v4 on v3

--- a/solution.py
+++ b/solution.py
@@ -37,7 +37,7 @@
     return -(-sum(run[4] for run in corner_runs(number, reach)) // 8)
 
 
-SUM_TILES = (7, 5, 7, 5, 2, 1, 1, 1)
+SUM_TILES = (8, 6, 8, 6, 2, 1, 1, 2)
 
 
 def iota(shape, dim):
@@ -140,7 +140,7 @@
     message2,
     message3,
     message4,
-    message_d2,
+    message7,
     arrive0,
     arrive1,
     arrive2,
@@ -294,16 +294,12 @@
     for half in (0, 8):
         cells[pl.ds(cell_row(-1, 7, 0, 0, 0) + half, 8), :] = zero_tile
 
-    pl.semaphore_wait(barrier, near_x * near_y - 1)
     loads[0].wait()
     loads[1].wait()
 
     for x in range(8):
         field_w[0, x + 5, 8:16] = flag_v[x].astype(F32)
     exchanges = halo(0, field_w, field_out, field_in, FIELD_REACH)
-    for copy in exchanges:
-        copy.start()
-
     for load in loads[2:7]:
         load.wait()
 
@@ -430,13 +426,19 @@
         message0[4 + i] = nodes[pl.ds((k * 9 + 7) * 8, 8), :]
     for i, k in enumerate((0, 2)):
         message2[4 + i] = nodes[pl.ds(k * 72 + 7, 8, stride=8), :]
+    field_f = flat_rows(field_w)
     message0[6] = d1
     message1[4] = d1
     message2[6] = d1
     message3[4] = d2
+    message0[7] = field_w[0, 12, 8:16]
+    message1[5] = field_w[0, 5, 8:16]
+    message2[7] = field_f[pl.ds(5 * 24 + 15, 8, stride=24), :]
+    message3[5] = field_f[pl.ds(5 * 24 + 8, 8, stride=24), :]
     message4[0] = d1
     message4[1] = d3
-    message_d2[0] = d2
+    message7[0] = d2
+    message7[1] = field_w[0, 5, 8:16]
 
     sums = [
         copy_to(number, 1, src, dst)
@@ -446,12 +448,16 @@
             (2, message2, arrive2),
             (3, message3, arrive3),
             (4, message4, arrive4),
-            (5, message_d2, arrive5),
+            (5, message7.at[pl.ds(0, 1)], arrive5),
             (6, message4.at[pl.ds(0, 1)], arrive6),
-            (7, message_d2, arrive7),
+            (7, message7, arrive7),
         )
     ]
+    pl.semaphore_wait(barrier, near_x * near_y - 1)
     for copy in sums:
+        copy.start()
+
+    for copy in exchanges:
         copy.start()
 
     loads[7].wait()
@@ -464,6 +470,103 @@
             lanes = pl.ds(pl.multiple_of(r * 128, 128), 128)
             slot_onehot[:, lanes] = matches(slot, 256)
         return carry
+
+    lax.fori_loop(0, 16, slot_rows, 0)
+
+    for copy in sums:
+        copy.wait_recv()
+
+    sub8 = iota((8, 128), 0)
+
+    def at_first(v, row):
+        return jnp.where(sub8 == 0, v + row, v)
+
+    speed_f = speed_w.reshape(3 * 10 * 24, 128)
+
+    def normalised(sums4, kind, dx, dy, components=(0, 1, 2)):
+        inverse = 1.0 / jnp.maximum(sums4[0], MASS_FLOOR)
+        result = []
+        for k in components:
+            u = sums4[k + 1] * inverse
+            if k == 2:
+                u = u - TIME_STEP * GRAVITY
+            result.append(kept(jnp.where(kind == 2.0, 0.0, u), dx, dy))
+        return result
+
+    minus_rows, below_columns = [None] * 4, [None] * 4
+    for i, k in enumerate((0, 1)):
+        minus_rows[k] = at_first(
+            kept(arrive0[4 + i], -1, 0), kept(arrive4[1, k : k + 1], -1, -1)
+        )
+    for i, k in enumerate((0, 2)):
+        below_columns[k] = at_first(
+            kept(arrive2[4 + i], 0, -1), kept(arrive4[1, 4 + k : 5 + k], -1, -1)
+        )
+    plus_rows, upper_columns = [], []
+    for k in range(4):
+        first = nodes[pl.ds(k * 72, 8), :] + kept(arrive0[k], -1, 0)
+        nodes[pl.ds(k * 72, 8), :] = first
+        column = at_first(
+            kept(arrive2[k], 0, -1), kept(arrive4[0, k : k + 1], -1, -1)
+        )
+        nodes[pl.ds(k * 72, 8, stride=8), :] = (
+            nodes[pl.ds(k * 72, 8, stride=8), :] + column
+        )
+        plus_rows.append(
+            at_first(
+                nodes[pl.ds((k * 9 + 8) * 8, 8), :] + kept(arrive1[k], 1, 0),
+                kept(arrive2[6, k : k + 1], 0, -1)
+                + kept(arrive6[0, 4 + k : 5 + k], 1, -1),
+            )
+        )
+        upper_columns.append(
+            at_first(
+                column8[k] + kept(arrive3[k], 0, 1),
+                kept(arrive0[6, k : k + 1], -1, 0) + kept(arrive5[0, k : k + 1], -1, 1),
+            )
+        )
+    corner = (
+        message4[0, 0:4]
+        + kept(arrive1[4, 4:8], 1, 0)
+        + kept(arrive3[4, 0:4], 0, 1)
+        + kept(arrive7[0, 4:8], 1, 1)
+    )
+
+    for x in range(-1, 9):
+        if x == -1:
+            sums4, side = minus_rows, -1
+        elif x == 8:
+            sums4, side = plus_rows, 1
+        else:
+            sums4 = [nodes[pl.ds((k * 9 + x) * 8, 8), :] for k in range(4)]
+            side = 0
+        wanted = (0,) if x == -1 else (0, 1, 2)
+        kind = {-1: arrive0[7], 1: arrive1[5], 0: field_w[0, x + 5, 8:16]}[side]
+        u = normalised(sums4, kind, side, 0, wanted)
+        for k in wanted:
+            speed_w[k, x + 1, 8:16] = u[k]
+    for columns, kind, y, side, wanted in (
+        (below_columns, arrive2[7], 7, -1, (1,)),
+        (upper_columns, arrive3[5], 16, 1, (0, 1, 2)),
+    ):
+        u = normalised(columns, kind, 0, side, wanted)
+        for i, k in enumerate(wanted):
+            speed_f[pl.ds((k * 10 + 1) * 24 + y, 8, stride=24), :] = u[i]
+    u = normalised([corner[k : k + 1] for k in range(4)], arrive7[1, 0:1], 1, 1)
+    for k in range(3):
+        speed_w[k, 9, 16:17] = u[k]
+
+    for x in range(8):
+        source_w[0, x + 5, 8:16] = 0.5 * (
+            speed_w[0, x + 2, 8:16]
+            - speed_w[0, x, 8:16]
+            + (speed_w[1, x + 1, 9:17] - speed_w[1, x + 1, 7:15])
+            + (above_z(speed_w[2, x + 1, 8:16]) - below_z(speed_w[2, x + 1, 8:16]))
+        )
+
+    margins = halo(2, source_w, source_out, source_in, SOURCE_REACH)
+    for copy in margins:
+        copy.start()
 
     for copy in exchanges:
         copy.wait_recv()
@@ -493,104 +596,6 @@
         )
         scale_w[x] = scale_w[x] / jnp.maximum(6.0 - closed, 1.0)
 
-    lax.fori_loop(0, 8, slot_rows, 0)
-
-    for copy in sums:
-        copy.wait_recv()
-
-    sub8 = iota((8, 128), 0)
-
-    def at_first(v, row):
-        return jnp.where(sub8 == 0, v + row, v)
-
-    speed_f = speed_w.reshape(3 * 10 * 24, 128)
-    field_f = flat_rows(field_w)
-
-    def normalised(sums4, kind, dx, dy, components=(0, 1, 2)):
-        inverse = 1.0 / jnp.maximum(sums4[0], MASS_FLOOR)
-        result = []
-        for k in components:
-            u = sums4[k + 1] * inverse
-            if k == 2:
-                u = u - TIME_STEP * GRAVITY
-            result.append(kept(jnp.where(kind == 2.0, 0.0, u), dx, dy))
-        return result
-
-    minus_rows, below_columns = [None] * 4, [None] * 4
-    for i, k in enumerate((0, 1)):
-        minus_rows[k] = at_first(
-            kept(arrive0[4 + i], -1, 0), kept(arrive4[1, k : k + 1], -1, -1)
-        )
-    for i, k in enumerate((0, 2)):
-        below_columns[k] = at_first(
-            kept(arrive2[4 + i], 0, -1), kept(arrive4[1, 4 + k : 5 + k], -1, -1)
-        )
-    plus_rows, upper_columns = [], []
-    for k in range(4):
-        first = nodes[pl.ds(k * 72, 8), :] + kept(arrive0[k], -1, 0)
-        nodes[pl.ds(k * 72, 8), :] = first
-        column = at_first(
-            kept(arrive2[k], 0, -1), kept(arrive4[0, k : k + 1], -1, -1)
-        )
-        nodes[pl.ds(k * 72, 8, stride=8), :] = (
-            nodes[pl.ds(k * 72, 8, stride=8), :] + column
-        )
-        plus_rows.append(
-            at_first(
-                nodes[pl.ds((k * 9 + 8) * 8, 8), :] + kept(arrive1[k], 1, 0),
-                kept(arrive2[6, k : k + 1], 0, -1)
-                + kept(arrive6[0, 4 + k : 5 + k], 1, -1),
-            )
-        )
-        upper_columns.append(
-            at_first(
-                column8[k] + kept(arrive3[k], 0, 1),
-                kept(arrive0[6, k : k + 1], -1, 0) + kept(arrive5[0, k : k + 1], -1, 1),
-            )
-        )
-    corner = (
-        message4[0, 0:4]
-        + kept(arrive1[4, 4:8], 1, 0)
-        + kept(arrive3[4, 0:4], 0, 1)
-        + kept(arrive7[0, 4:8], 1, 1)
-    )
-
-    for x in range(-1, 9):
-        if x == -1:
-            sums4, side = minus_rows, -1
-        elif x == 8:
-            sums4, side = plus_rows, 1
-        else:
-            sums4 = [nodes[pl.ds((k * 9 + x) * 8, 8), :] for k in range(4)]
-            side = 0
-        wanted = (0,) if x == -1 else (0, 1, 2)
-        u = normalised(sums4, field_w[0, x + 5, 8:16], side, 0, wanted)
-        for k in wanted:
-            speed_w[k, x + 1, 8:16] = u[k]
-    for columns, y, side, wanted in (
-        (below_columns, 7, -1, (1,)),
-        (upper_columns, 16, 1, (0, 1, 2)),
-    ):
-        kind = field_f[pl.ds(5 * 24 + y, 8, stride=24), :]
-        u = normalised(columns, kind, 0, side, wanted)
-        for i, k in enumerate(wanted):
-            speed_f[pl.ds((k * 10 + 1) * 24 + y, 8, stride=24), :] = u[i]
-    u = normalised([corner[k : k + 1] for k in range(4)], field_w[0, 13, 16:17], 1, 1)
-    for k in range(3):
-        speed_w[k, 9, 16:17] = u[k]
-
-    for x in range(8):
-        source_w[0, x + 5, 8:16] = 0.5 * (
-            speed_w[0, x + 2, 8:16]
-            - speed_w[0, x, 8:16]
-            + (speed_w[1, x + 1, 9:17] - speed_w[1, x + 1, 7:15])
-            + (above_z(speed_w[2, x + 1, 8:16]) - below_z(speed_w[2, x + 1, 8:16]))
-        )
-
-    margins = halo(2, source_w, source_out, source_in, SOURCE_REACH)
-    for copy in margins:
-        copy.start()
-    lax.fori_loop(8, 16, slot_rows, 0)
     for copy in margins:
         copy.wait_recv()
     unpack(source_w, source_in, SOURCE_REACH)
@@ -839,12 +844,12 @@
             f32(10 * 10 * 16, 128),
             f32(4 * 9 * 8, 128),
             f32(4, 8, 128),
-            f32(7, 8, 128),
-            f32(5, 8, 128),
-            f32(7, 8, 128),
-            f32(5, 8, 128),
+            f32(8, 8, 128),
+            f32(6, 8, 128),
+            f32(8, 8, 128),
+            f32(6, 8, 128),
             f32(2, 8, 128),
-            f32(1, 8, 128),
+            f32(2, 8, 128),
         ]
         + [f32(tiles, 8, 128) for tiles in SUM_TILES]
         + [

time: 30.8 us -> 30.3 us (0.984)
  the two profiles are of different devices: /device:TPU:231 before, /device:TPU:239 now
where the time goes in v4:
time: 30.3 us; the launch traced here: 30.1 us
  Pallas kernels  29.5 us (97%)
  between operations  0.64 us (2%)
    pallas_call x1, Pallas kernels, on_device(): pl.pallas_call(functools.partial(kernel, nx, ny), out_shape=[pltpu.VMEM(s...  28.6 us
    pallas_call x1, Pallas kernels, on_device(): pl.pallas_call(write_out, out_shape=[jax.ShapeDtypeStruct(shape, F32) for...  0.87 us

profile of v4, /device:TPU:239, one launch (start us, length us, event | category | flops | bytes accessed | tf_op | source)
XLA Modules:
  0.0 30.1 jit_solution(5162083016227019762)
XLA Ops:
  0.6 28.6 %substep.1 = (f32[3,64,128]{2,1,0:T(8,128)S(1)}, f32[3,64,128]{2,1,0:T(8,128)S(1)}, f32[9,64,128]{2,1,0:T(8,128)S(1)}, f32[8,8,128]{2,1,0:T(8,128)S(1)}, f32[15,16,128]{2,1,0:T(8,128)S(1)}) custom-call(f32[3,64,128]{2,1,0:T(8,128)} %bitcast.47, f32[3,64,128]{2,1,0:T(8,128)} %bitcast.48, f32[9,64,128]{2,1,0:T(8,128)} %bitcast.46, s32[64,128]{1,0:T(8,128)} %bitcast.49, ...), custom_call_target="tpu_custom_call" | custom-call | tf_op jit(solution)/shard_map/substep/pallas_call | solution.py:825
  29.2 0.9 %write_out.1 = (f32[3,64,128]{2,1,0:T(8,128)}, f32[3,64,128]{2,1,0:T(8,128)}, f32[9,64,128]{2,1,0:T(8,128)}, f32[8,8,128]{2,1,0:T(8,128)}, f32[15,16,128]{2,1,0:T(8,128)}) custom-call(f32[3,64,128]{2,1,0:T(8,128)S(1)} %get-tuple-element.15.refs_0_, f32[3,64,128]{2,1,0:T(8,128)S(1)} %get-tuple-element.16.refs_1_, ...), custom_call_target="tpu_custom_call" | custom-call | tf_op jit(solution)/shard_map/write_out/pallas_call | solution.py:897
